TPU v7x, 1024 devices: a whole 4x8x16 slice. The times are simulated.
1024 devices in a mesh: tile: 128 (over y, z_lo, core), strip: 8 (over x, z_hi).
Axes of the slice: x: 4, y: 8, z: 16 (z_hi: 2, z_lo: 8; z = z_hi * 8 + z_lo), core: 2. Of those that a mesh axis runs over, the one named last changes fastest.
Arguments:
- fine_cotangent: float32 [70, 512, 4096], P(None, 'tile', 'strip'), may hold values from -6 to 6
- middle_cotangent: float32 [70, 256, 2048], P(None, 'tile', 'strip'), may hold values from -12 to 12
- coarse_cotangent: float32 [70, 128, 1024], P(None, 'tile', 'strip'), may hold values from -24 to 24
- fine_shift: float32 [70, 512, 4096], P(None, 'tile', 'strip'), may hold values from 0.5 to 2
- middle_shift: float32 [70, 256, 2048], P(None, 'tile', 'strip'), may hold values from 0.5 to 2
- coarse_shift: float32 [70, 128, 1024], P(None, 'tile', 'strip'), may hold values from 0.5 to 2
- lower_coupling: float32 [70], replicated, may hold values from 0.4 to 1
- upper_coupling: float32 [70], replicated, may hold values from 0.4 to 1
- seam_flip: int32 [128], replicated, may hold values from 0 to 1
Outputs:
- adjoint_field: float32 [70, 512, 4096], P(None, 'tile', 'strip')
All inputs are finite; a program needn't handle non-finite values.
Results may differ from a plain program's by a relative error of at most 0.00002.
Values sent between devices are 32-bit elements; how exact they have to be, the bound alone decides.
No kernel may reach another device: no remote copies, remote signals or barrier semaphores. Data moves between devices by JAX's collectives and lax.ppermute only.
A program may use at most 128 MiB of HBM per device.

v0:
```python
import jax
import jax.numpy as jnp
from jax import lax
from jax.sharding import PartitionSpec as P


def passed_along(array, axis, by):
    devices = lax.axis_size(axis)
    return lax.ppermute(array, axis, [(i, (i + by) % devices) for i in range(devices)])


def padded_2(cells, sides, width):
    for axis, dim in sides:
        count = lax.axis_size(axis)
        ends = count - 1
        head = lax.slice_in_dim(cells, 0, width, axis=dim)
        tail = lax.slice_in_dim(cells, cells.shape[dim] - width, cells.shape[dim], axis=dim)
        cells = jnp.concatenate(
            [
                lax.ppermute(tail, axis, [(i, (i + 1) % count) for i in range(ends)]),
                cells,
                lax.ppermute(head, axis, [((i + 1) % count, i) for i in range(ends)]),
            ],
            axis=dim,
        )
    return cells


def transposed_solve(rhs, shift, lower_coupling, upper_coupling):
    depth = rhs.shape[0]
    shape_rest = rhs.shape[1:]
    flat_rhs = rhs.reshape(depth, -1)
    flat_shift = shift.reshape(depth, -1)
    zero_one = jnp.zeros((1,), jnp.float32)
    lower_terms = jnp.concatenate([zero_one, -upper_coupling[:-1]])
    upper_terms = jnp.concatenate([-lower_coupling[1:], zero_one])
    diagonal = (lower_coupling + upper_coupling)[:, None] + flat_shift
    factor = jnp.zeros(flat_rhs.shape[1:], jnp.float32)
    partial_value = jnp.zeros(flat_rhs.shape[1:], jnp.float32)
    factors = []
    partials = []
    for level in range(depth):
        pivot = diagonal[level] - lower_terms[level] * factor
        factor = upper_terms[level] / pivot
        partial_value = (flat_rhs[level] - lower_terms[level] * partial_value) / pivot
        factors.append(factor)
        partials.append(partial_value)
    solved = jnp.zeros(flat_rhs.shape[1:], jnp.float32)
    outputs = [None] * depth
    for level in range(depth - 1, -1, -1):
        solved = partials[level] - factors[level] * solved
        outputs[level] = solved
    return jnp.stack(outputs, axis=0).reshape((depth,) + shape_rest)


def spread_rows(field, seam_flip):
    depth, height, width = field.shape
    position = lax.axis_index("tile")
    count = lax.axis_size("tile")
    flip_before = seam_flip[(position + count - 1) % count]
    flip_after = seam_flip[position]
    before_row = passed_along(field[:, -1], "tile", 1)
    after_row = passed_along(field[:, 0], "tile", -1)
    before_row = jnp.where(flip_before == 1, before_row[:, ::-1], before_row)
    after_row = jnp.where(flip_after == 1, after_row[:, ::-1], after_row)
    upward_rows = jnp.concatenate([before_row[:, None], field[:, :-1]], axis=1)
    downward_rows = jnp.concatenate([field[:, 1:], after_row[:, None]], axis=1)
    even_rows = 0.375 * field + 0.125 * upward_rows
    odd_rows = 0.375 * field + 0.125 * downward_rows
    return jnp.stack([even_rows, odd_rows], axis=2).reshape(depth, 2 * height, width)


def spread_columns(field):
    depth, height, width = field.shape
    padded = padded_2(field, (("strip", 2),), 1)
    even_cols = 0.375 * field + 0.125 * padded[:, :, :-2]
    odd_cols = 0.375 * field + 0.125 * padded[:, :, 2:]
    return jnp.stack([even_cols, odd_cols], axis=-1).reshape(depth, height, 2 * width)


def level_step(cotangent, shift, coarser, lower_coupling, upper_coupling, seam_flip):
    carried = spread_columns(spread_rows(coarser, seam_flip))
    return transposed_solve(cotangent + carried, shift, lower_coupling, upper_coupling)


def on_device(
    fine_cotangent,
    middle_cotangent,
    coarse_cotangent,
    fine_shift,
    middle_shift,
    coarse_shift,
    lower_coupling,
    upper_coupling,
    seam_flip,
):
    coarse_solved = transposed_solve(coarse_cotangent, coarse_shift, lower_coupling, upper_coupling)
    middle_solved = level_step(
        middle_cotangent, middle_shift, coarse_solved, lower_coupling, upper_coupling, seam_flip
    )
    return level_step(
        fine_cotangent, fine_shift, middle_solved, lower_coupling, upper_coupling, seam_flip
    )


def solution(mesh):
    in_specs = (
        P(None, "tile", "strip"),
        P(None, "tile", "strip"),
        P(None, "tile", "strip"),
        P(None, "tile", "strip"),
        P(None, "tile", "strip"),
        P(None, "tile", "strip"),
        P(),
        P(),
        P(),
    )
    out_specs = P(None, "tile", "strip")
    return jax.shard_map(
        on_device, mesh=mesh, in_specs=in_specs, out_specs=out_specs, check_vma=False
    )
```

profile of v0, /device:TPU:36, one launch (start us, length us, event | category | flops | bytes accessed | tf_op | source)
XLA Modules:
  0.0 834.9 jit_solution(338638529753947781)
XLA Ops:
  6.6 51.9 %broadcast_divide_fusion.208 = (f32[1,128]{1,0:T(1,128)S(1)}, f32[1,128]{1,0:T(1,128)S(1)}, f32[1,128]{1,0:T(1,128)S(1)}, f32[1,128]{1,0:T(1,128)S(1)}, f32[1,12...) fusion(f32[]{:T(128)} %bitcast.166, ...), kind=kLoop, calls=%fused_computation.1491 | loop fusion | flops 15872 | bytes 40780 | tf_op jit(solution)/shard_map/div | solution.py:44
  59.3 86.5 %fusion.152 = (f32[1,128]{1,0:T(1,128)S(1)}, f32[128]{0:T(128)S(1)}, f32[128]{0:T(128)S(1)}, f32[128]{0:T(128)S(1)}, f32[128]{0:T(128)S(1)}, /*index=5*/f32[128]...) fusion(f32[70,128]{1,0:T(8,128)S(1)} %bitcast_add_fusion, ...), kind=kLoop, calls=%fused_computation.1594 | loop fusion | flops 53760 | bytes 143912 | tf_op jit(solution)/shard_map/stack | solution.py:53
  146.2 28.7 %fusion.42 = (f32[1,128]{1,0:T(1,128)S(1)}, f32[1,128]{1,0:T(1,128)S(1)}, f32[1,128]{1,0:T(1,128)S(1)}, f32[1,128]{1,0:T(1,128)S(1)}, f32[1,128]{1,0:T(1,128)S(1...) fusion(f32[70,1,128]{2,1,0:T(1,128)S(1)} %copy-done.3, ...), kind=kLoop, calls=%fused_computation.1086 | loop fusion | flops 26496 | bytes 78520 | tf_op jit(solution)/shard_map/div | solution.py:45
  174.9 34.8 %multiply_subtract_fusion.357 = (f32[1,128]{1,0:T(1,128)S(1)}, f32[1,128]{1,0:T(1,128)S(1)}, f32[1,128]{1,0:T(1,128)S(1)}, f32[1,128]{1,0:T(1,128)S(1)}, f32[1,1...) fusion(f32[1,128]{1,0:T(1,128)S(1)} %get-tuple-element.881, ...), kind=kLoop, calls=%fused_computation.1377 | loop fusion | flops 37632 | bytes 83164 | tf_op jit(solution)/shard_map/sub | solution.py:51
  211.9 15.7 %collective-permute-start.1 = (f32[70,128]{1,0:T(8,128)S(1)}, f32[70,128]{1,0:T(8,128)S(1)}, u32[]{:S(2)}, u32[]{:S(2)}) collective-permute-start(f32[70,128]{1,0:T(8,128)S(1)} %stack.775), channel_id=1, source_target_pairs={{0,1016},{8,0},{16,8},{24,16},{32,24},{40,32},{48,40},{56,48},{64,... | collective-permute-start | bytes 107528 | tf_op jit(solution)/shard_map/ppermute | solution.py:9
  233.0 16.0 %collective-permute-start.2 = (f32[70,2,1]{2,0,1:T(8,128)S(1)}, f32[70,2,1]{2,0,1:T(8,128)S(1)}, u32[]{:S(2)}, u32[]{:S(2)}) collective-permute-start(f32[70,2,1]{2,0,1:T(8,128)S(1)} %get-tuple-element.1041), channel_id=1, source_target_pairs={{0,1},{1,2},{2,3},{3,4},{4,5},{5,6},{6,7},{8,9},{9,10},{10,11},{11... | collective-permute-start | bytes 1688 | tf_op jit(solution)/shard_map/ppermute | solution.py:20
  251.1 8.6 %multiply_subtract_fusion.248 = (f32[1,512]{1,0:T(1,128)S(1)}, f32[1,512]{1,0:T(1,128)S(1)}, f32[1,512]{1,0:T(1,128)S(1)}) fusion(f32[]{:T(128)} %bitcast.26, f32[]{:T(128)} %bitcast.28, f32[70,512]{1,0:T(8,128)S(1)} %broadcast_add_fusion.1, f32[]{:T(128)} %bitcast.22, f32[]{:T(128)} %bitcast.24, f32[]{:T(128)} %bitcast.14, f32[]{:T(128)} %bitcast.16, ...), kind=kLoop, calls=%fused_computation.741 | loop fusion | flops 10752 | bytes 22584 | tf_op jit(solution)/shard_map/sub | solution.py:43
  275.9 7.4 subtract_divide_fusion.212
  283.3 49.5 %subtract_divide_fusion.109 = (f32[1,512]{1,0:T(1,128)S(1)}, f32[1,512]{1,0:T(1,128)S(1)}, f32[1,512]{1,0:T(1,128)S(1)}, f32[1,512]{1,0:T(1,128)S(1)}, f32[1,512...) fusion(f32[1,512]{1,0:T(1,128)S(1)} %bitcast.3487, ...), kind=kLoop, calls=%fused_computation.674 | loop fusion | flops 121856 | bytes 313660 | tf_op jit(solution)/shard_map/div | solution.py:45
  332.8 79.0 %subtract_divide_fusion.150 = (f32[512]{0:T(512)S(1)}, f32[512]{0:T(512)S(1)}, f32[512]{0:T(512)S(1)}, f32[512]{0:T(512)S(1)}, f32[512]{0:T(512)S(1)}, /*index=5...) fusion(f32[512]{0:T(512)S(1)} %bitcast.3505, ...), kind=kLoop, calls=%fused_computation.790 | loop fusion | flops 191488 | bytes 422388 | tf_op jit(solution)/shard_map/div | solution.py:45
  411.8 30.8 %multiply_subtract_fusion.255 = (f32[512]{0:T(512)S(1)}, f32[512]{0:T(512)S(1)}, f32[512]{0:T(512)S(1)}, f32[512]{0:T(512)S(1)}, f32[512]{0:T(512)S(1)}, /*index...) fusion(f32[512]{0:T(512)S(1)} %get-tuple-element.609, ...), kind=kLoop, calls=%fused_computation.755 | loop fusion | flops 155136 | bytes 374980 | tf_op jit(solution)/shard_map/sub | solution.py:51
  442.6 35.9 %multiply_subtract_fusion.178 = (f32[1,512]{1,0:T(1,128)S(1)}, f32[1,512]{1,0:T(1,128)S(1)}, f32[1,512]{1,0:T(1,128)S(1)}, f32[1,512]{1,0:T(1,128)S(1)}, f32[1,5...) fusion(f32[1,512]{1,0:T(1,128)S(1)} %get-tuple-element.481, ...), kind=kLoop, calls=%fused_computation.637 | loop fusion | flops 152064 | bytes 332004 | tf_op jit(solution)/shard_map/sub | solution.py:51
  478.9 7.7 collective-permute-start.5
  486.6 9.2 %multiply_subtract_fusion.69 = (f32[1,2048]{1,0:T(1,128)}, f32[1,2048]{1,0:T(1,128)}, f32[1,2048]{1,0:T(1,128)}) fusion(f32[]{:T(128)} %bitcast.26, f32[]{:T(128)} %bitcast.28, f32[70,2048]{1,0:T(8,128)S(1)} %broadcast_add_fusion, f32[]{:T(128)} %bitcast.22, f32[]{:T(128)} %bitcast.24, f32[]{:T(128)} %bitcast.14, f32[]{:T(128)} %bitcast.16, f32[]{:T(128)} %bitcast.18, ...), kind=kLoop, calls=%fused_computation.349 | loop fusion | flops 43008 | bytes 90168 | tf_op jit(solution)/shard_map/sub | solution.py:43
  498.3 26.7 %collective-permute-done.4 = f32[70,256]{1,0:T(8,128)S(1)} collective-permute-done((f32[70,256]{1,0:T(8,128)S(1)}, f32[70,256]{1,0:T(8,128)S(1)}, u32[]{:S(2)}, u32[]{:S(2)}) %collective-permute-start.4) | collective-permute-done | bytes 71712 | tf_op jit(solution)/shard_map/ppermute | solution.py:9
  525.3 8.4 %collective-permute-start.6 = (f32[70,4,1]{2,0,1:T(8,128)S(1)}, f32[70,4,1]{2,0,1:T(8,128)S(1)}, u32[]{:S(2)}, u32[]{:S(2)}) collective-permute-start(f32[70,4,1]{2,0,1:T(8,128)S(1)} %get-tuple-element.961), channel_id=1, source_target_pairs={{0,1},{1,2},{2,3},{3,4},{4,5},{5,6},{6,7},{8,9},{9,10},{10,11},{11... | collective-permute-start | bytes 3368 | tf_op jit(solution)/shard_map/ppermute | solution.py:20
  533.7 7.2 collective-permute-start.7
  541.0 20.1 %broadcast_divide_fusion.88 = (f32[2048]{0:T(1024)}, f32[2048]{0:T(1024)}, f32[2048]{0:T(1024)}, f32[2048]{0:T(1024)}, f32[2048]{0:T(1024)}, /*index=5*/f32[2048]{0:T(1024)}, f32[2048]{0:T(1024)}, f32[2048]{0:T(1024)}) fusion(f32[]{:T(128)} %bitcast.62, f32[2048]{0:T(1024)S(1)} %bitcast.2537, f32[]{:T(128)} %bitcast.60, f32[2048]{0:T(1024)S(1)} %bitcast.2540, ...), kind=kLoop, calls=%fused_computation.621 | loop fusion | flops 94208 | bytes 196732 | tf_op jit(solution)/shard_map/div | solution.py:44
  562.5 10.5 %slice_reduce_fusion.40 = (f32[4,512]{1,0:T(4,128)S(1)}, f32[4,512]{1,0:T(4,128)S(1)}, f32[4,512]{1,0:T(4,128)S(1)}, f32[4,512]{1,0:T(4,128)S(1)}, f32[4,512]{1,...) fusion(f32[70,4,512]{0,2,1:T(8,128)S(1)} %add.110), kind=kLoop, calls=%fused_computation.40 | loop fusion | bytes 311296 | tf_op jit(solution)/shard_map/slice | solution.py:45
  573.0 10.5 %slice_reduce_fusion.19 = (f32[4,512]{1,0:T(4,128)S(1)}, f32[4,512]{1,0:T(4,128)S(1)}, f32[4,512]{1,0:T(4,128)S(1)}, f32[4,512]{1,0:T(4,128)S(1)}, f32[4,512]{1,...) fusion(f32[70,4,512]{0,2,1:T(8,128)S(1)} %add.110), kind=kLoop, calls=%fused_computation.19 | loop fusion | bytes 311296 | tf_op jit(solution)/shard_map/slice | solution.py:45
  583.5 10.7 %slice_reduce_fusion = (f32[4,512]{1,0:T(4,128)S(1)}, f32[4,512]{1,0:T(4,128)S(1)}, f32[4,512]{1,0:T(4,128)S(1)}, f32[4,512]{1,0:T(4,128)S(1)}, f32[4,512]{1,0:T...) fusion(f32[70,4,512]{0,2,1:T(8,128)S(1)} %add.110), kind=kLoop, calls=%fused_computation | loop fusion | bytes 311296 | tf_op jit(solution)/shard_map/slice | solution.py:45
  603.1 86.8 %fusion.185 = (f32[2048]{0:T(1024)S(1)}, f32[2048]{0:T(1024)S(1)}, f32[1,2048]{1,0:T(1,128)S(1)}, f32[1,2048]{1,0:T(1,128)S(1)}, f32[1,2048]{1,0:T(1,128)S(1)}, ...) fusion(f32[]{:T(128)} %broadcast.23065, ...), kind=kLoop, calls=%fused_computation.1627 | loop fusion | flops 952320 | bytes 1745440 | tf_op jit(solution)/shard_map/sub | solution.py:51
  707.8 78.4 %subtract_divide_fusion.41 = (f32[2048]{0:T(1024)S(1)}, f32[2048]{0:T(1024)S(1)}, f32[2048]{0:T(1024)S(1)}, f32[2048]{0:T(1024)S(1)}, f32[2048]{0:T(1024)S(1)}, ...) fusion(f32[2048]{0:T(1024)S(1)} %bitcast.2896, ...), kind=kLoop, calls=%fused_computation.398 | loop fusion | flops 765952 | bytes 1548776 | tf_op jit(solution)/shard_map/div | solution.py:45
  786.9 44.7 %multiply_subtract_fusion.76 = (f32[2048]{0:T(1024)S(1)}, f32[2048]{0:T(1024)S(1)}, f32[2048]{0:T(1024)S(1)}, f32[2048]{0:T(1024)S(1)}, f32[2048]{0:T(1024)S(1)}...) fusion(f32[2048]{0:T(1024)S(1)} %get-tuple-element.376, ...), kind=kLoop, calls=%fused_computation.363 | loop fusion | flops 720896 | bytes 1466652 | tf_op jit(solution)/shard_map/sub | solution.py:51
  (643 shorter events, 63.9 us)
Async XLA Ops:
  174.9 52.7 %copy-start.4 = (f32[70,2,256]{2,1,0:T(2,128)S(1)}, f32[70,2,256]{2,1,0:T(2,128)}, u32[]{:S(2)}) copy-start(f32[70,2,256]{2,1,0:T(2,128)} %param.13) | copy-start | bytes 430084
  209.9 18.0 %copy-start.1 = (f32[70,4,512]{2,1,0:T(4,128)S(1)}, f32[70,4,512]{2,1,0:T(4,128)}, u32[]{:S(2)}) copy-start(f32[70,4,512]{2,1,0:T(4,128)} %param.12) | copy-start | bytes 1720324
  209.9 22.8 %collective-permute-start = (f32[70,128]{1,0:T(8,128)S(1)}, f32[70,128]{1,0:T(8,128)S(1)}, u32[]{:S(2)}, u32[]{:S(2)}) collective-permute-start(f32[70,128]{1,0:T(8,128)S(1)} %stack.775), channel_id=1, source_target_pairs={{0,8},{8,16},{16,24},{24,32},{32,40},{40,48},{48,56},{56,64},{64,7... | collective-permute-start | bytes 107528 | tf_op jit(solution)/shard_map/ppermute | solution.py:9
  211.9 20.8 %collective-permute-start.1 = (f32[70,128]{1,0:T(8,128)S(1)}, f32[70,128]{1,0:T(8,128)S(1)}, u32[]{:S(2)}, u32[]{:S(2)}) collective-permute-start(f32[70,128]{1,0:T(8,128)S(1)} %stack.775), channel_id=1, source_target_pairs={{0,1016},{8,0},{16,8},{24,16},{32,24},{40,32},{48,40},{56,48},{64,... | collective-permute-start | bytes 107528 | tf_op jit(solution)/shard_map/ppermute | solution.py:9
  228.5 312.4 %copy-start.17 = (f32[1,2048]{1,0:T(1,128)}, f32[1,2048]{1,0:T(1,128)S(1)}, u32[]{:S(2)}) copy-start(f32[1,2048]{1,0:T(1,128)S(1)} %get-tuple-element.953) | copy-start | bytes 24580
  228.5 312.4 %copy-start.19 = (f32[1,2048]{1,0:T(1,128)}, f32[1,2048]{1,0:T(1,128)S(1)}, u32[]{:S(2)}) copy-start(f32[1,2048]{1,0:T(1,128)S(1)} %get-tuple-element.954) | copy-start | bytes 24580
  228.6 312.4 %copy-start.21 = (f32[1,2048]{1,0:T(1,128)}, f32[1,2048]{1,0:T(1,128)S(1)}, u32[]{:S(2)}) copy-start(f32[1,2048]{1,0:T(1,128)S(1)} %get-tuple-element.955) | copy-start | bytes 24580
  228.6 312.4 %copy-start.23 = (f32[1,2048]{1,0:T(1,128)}, f32[1,2048]{1,0:T(1,128)S(1)}, u32[]{:S(2)}) copy-start(f32[1,2048]{1,0:T(1,128)S(1)} %get-tuple-element.956) | copy-start | bytes 24580
  228.6 312.4 %copy-start.25 = (f32[1,2048]{1,0:T(1,128)}, f32[1,2048]{1,0:T(1,128)S(1)}, u32[]{:S(2)}) copy-start(f32[1,2048]{1,0:T(1,128)S(1)} %get-tuple-element.957) | copy-start | bytes 24580
  228.6 312.4 %copy-start.27 = (f32[1,2048]{1,0:T(1,128)}, f32[1,2048]{1,0:T(1,128)S(1)}, u32[]{:S(2)}) copy-start(f32[1,2048]{1,0:T(1,128)S(1)} %get-tuple-element.958) | copy-start | bytes 24580
  232.9 26.8 %copy-start.2 = (f32[70,2,256]{2,1,0:T(2,128)S(1)}, f32[70,2,256]{2,1,0:T(2,128)}, u32[]{:S(2)}) copy-start(f32[70,2,256]{2,1,0:T(2,128)} %param.10) | copy-start | bytes 430084
  233.0 26.9 %collective-permute-start.2 = (f32[70,2,1]{2,0,1:T(8,128)S(1)}, f32[70,2,1]{2,0,1:T(8,128)S(1)}, u32[]{:S(2)}, u32[]{:S(2)}) collective-permute-start(f32[70,2,1]{2,0,1:T(8,128)S(1)} %get-tuple-element.1041), channel_id=1, source_target_pairs={{0,1},{1,2},{2,3},{3,4},{4,5},{5,6},{6,7},{8,9},{9,10},{10,11},{11... | collective-permute-start | bytes 1688 | tf_op jit(solution)/shard_map/ppermute | solution.py:20
  249.0 15.0 %collective-permute-start.3 = (f32[70,2,1]{2,0,1:T(8,128)S(1)}, f32[70,2,1]{2,0,1:T(8,128)S(1)}, u32[]{:S(2)}, u32[]{:S(2)}) collective-permute-start(f32[70,2,1]{2,0,1:T(8,128)S(1)} %get-tuple-element.1042), channel_id=1, source_target_pairs={{1,0},{2,1},{3,2},{4,3},{5,4},{6,5},{7,6},{9,8},{10,9},{11,10},{12... | collective-permute-start | bytes 1688 | tf_op jit(solution)/shard_map/ppermute | solution.py:22
  478.9 19.2 %collective-permute-start.5 = (f32[70,256]{1,0:T(8,128)S(1)}, f32[70,256]{1,0:T(8,128)S(1)}, u32[]{:S(2)}, u32[]{:S(2)}) collective-permute-start(f32[70,256]{1,0:T(8,128)S(1)} %get-tuple-element.967), channel_id=1, source_target_pairs={{0,1016},{8,0},{16,8},{24,16},{32,24},{40,32},{48,40},{56,48},{64,... | collective-permute-start | bytes 215048 | tf_op jit(solution)/shard_map/ppermute | solution.py:9
  495.8 29.1 %collective-permute-start.4 = (f32[70,256]{1,0:T(8,128)S(1)}, f32[70,256]{1,0:T(8,128)S(1)}, u32[]{:S(2)}, u32[]{:S(2)}) collective-permute-start(f32[70,256]{1,0:T(8,128)S(1)} %get-tuple-element.965), channel_id=1, source_target_pairs={{0,8},{8,16},{16,24},{24,32},{32,40},{40,48},{48,56},{56,64},{64,7... | collective-permute-start | bytes 215048 | tf_op jit(solution)/shard_map/ppermute | solution.py:9
  525.2 35.8 %copy-start = (f32[70,4,512]{2,1,0:T(4,128)S(1)}, f32[70,4,512]{2,1,0:T(4,128)}, u32[]{:S(2)}) copy-start(f32[70,4,512]{2,1,0:T(4,128)} %param.9) | copy-start | bytes 1720324
  525.3 36.1 %collective-permute-start.6 = (f32[70,4,1]{2,0,1:T(8,128)S(1)}, f32[70,4,1]{2,0,1:T(8,128)S(1)}, u32[]{:S(2)}, u32[]{:S(2)}) collective-permute-start(f32[70,4,1]{2,0,1:T(8,128)S(1)} %get-tuple-element.961), channel_id=1, source_target_pairs={{0,1},{1,2},{2,3},{3,4},{4,5},{5,6},{6,7},{8,9},{9,10},{10,11},{11... | collective-permute-start | bytes 3368 | tf_op jit(solution)/shard_map/ppermute | solution.py:20
  533.7 27.7 %collective-permute-start.7 = (f32[70,4,1]{2,0,1:T(8,128)S(1)}, f32[70,4,1]{2,0,1:T(8,128)S(1)}, u32[]{:S(2)}, u32[]{:S(2)}) collective-permute-start(f32[70,4,1]{2,0,1:T(8,128)S(1)} %get-tuple-element.962), channel_id=1, source_target_pairs={{1,0},{2,1},{3,2},{4,3},{5,4},{6,5},{7,6},{9,8},{10,9},{11,10},{12... | collective-permute-start | bytes 3368 | tf_op jit(solution)/shard_map/ppermute | solution.py:22
  702.1 5.0 copy-start.8
  702.2 5.0 copy-start.9
  702.2 5.0 copy-start.10
  702.2 5.0 copy-start.11
  702.2 5.0 copy-start.12
  702.2 5.0 copy-start.18
  (44 other events, 128.3 us)
where the time goes:
time: 849 us; the launch traced here: 835 us
  other arithmetic  669 us (79%)
  local copies, waits for them, and re-layouts  68.1 us (8%)
  starting transfers between devices  61.1 us (7%)
  waiting for transfers between devices  30.8 us (4%)
    div x6, other arithmetic, transposed_solve(): (flat_rhs[level] - lower_terms[level] * partial_value) / pivot  247 us
    sub x22, other arithmetic, transposed_solve(): solved = partials[level] - factors[level] * solved  244 us
    another operation x17, other arithmetic, transposed_solve(): return jnp.stack(outputs, axis=0).reshape((depth,) + shape_rest)  86.8 us
    div x2, other arithmetic, transposed_solve(): factor = upper_terms[level] / pivot  71.9 us
    slice x8, local copies, waits for them, and re-layouts, transposed_solve(): flat_rhs[level] - lower_terms[level] * partial_value  48.6 us
    ppermute x4, starting transfers between devices, passed_along(): lax.ppermute(array, axis, [(i, (i + by) % devices) for i in range(devices)])  27.3 us
    ppermute x4, waiting for transfers between devices, passed_along(): lax.ppermute(array, axis, [(i, (i + by) % devices) for i in range(devices)])  26.7 us
    ppermute x2, starting transfers between devices, padded_2(): lax.ppermute(tail, axis, [(i, (i + 1) % count) for i in range(ends)])  24.4 us
  transfers between devices with their start and end apart: 8, of which 2 were waited for; matrix products, arithmetic and copies ran while one was open for 5% of the time, Pallas kernels for 0%

commit v1 on v0

v1 whole, which is shorter than its diff:
```python
import functools

import jax
import jax.numpy as jnp
import ml_dtypes
import numpy as np
from jax import lax
from jax.experimental import pallas as pl
from jax.experimental.pallas import tpu as pltpu
from jax.sharding import PartitionSpec as P

LANES = 128
GROUP = 14
PACK_LIMIT = 60 * 1024 * 1024
EDGES = 6
BOTH = ("tile", "strip")
VMEM = pl.BlockSpec(memory_space=pltpu.VMEM)
SMEM = pl.BlockSpec(memory_space=pltpu.SMEM)
ANY = pl.BlockSpec(memory_space=pl.ANY)


def edge_lane(a, b, e):
    return ((a + 1) * 5 + b + 2) * EDGES + e


def edge_maps():
    halo = 96
    to_middle = np.zeros((2, 2, LANES, LANES))
    to_fine = np.zeros((2, 2, LANES, LANES))
    for before in (0, 1):
        for after in (0, 1):
            w1, w2 = to_middle[before, after], to_fine[before, after]

            def spread(a, r, b, j):
                other, flip = {(-1, 1): (0, before), (0, 0): (-1, before), (0, 1): (1, after), (1, 0): (0, after)}[a, r]
                return [(edge_lane(a, b, j), 0.375), (edge_lane(other, b, 1 - j if flip else j), 0.125)]

            def put(w, terms, scale, out):
                for lane, weight in terms:
                    w[lane, out] += scale * weight

            rows = [(-1, 1, before), (0, 0, 0), (0, 1, 0), (1, 0, after)]
            for i, (a, r, flip) in enumerate(rows):
                for b in (-1, 1):
                    out = edge_lane(a, b, 2 + 2 * r)
                    put(w1, spread(a, r, b, 0), 0.375, out)
                    put(w1, spread(a, r, b - 1, 1), 0.125, out)
                    put(w1, spread(a, r, b, 1), 0.375, out + 1)
                    put(w1, spread(a, r, b + 1, 0), 0.125, out + 1)
                put(w1, spread(a, r, -1, 1), 1.0, halo + 2 * i + (1 if flip else 0))
                put(w1, spread(a, r, 1, 0), 1.0, halo + 2 * i + (0 if flip else 1))

            def cell(row, side):
                a, r, flip = rows[row]
                last = (side == 0) != bool(flip)
                return edge_lane(a, -1 if side == 0 else 1, 2 + 2 * r + (1 if last else 0))

            for i, (main, other) in enumerate(((1, 0), (1, 2), (2, 1), (2, 3))):
                for side in (0, 1):
                    w2[cell(main, side), 2 * i + side] += 0.375
                    w2[cell(other, side), 2 * i + side] += 0.125
    both = np.stack([to_middle.reshape(4, LANES, LANES), to_fine.reshape(4, LANES, LANES)])
    return both.reshape(8, LANES, LANES).astype(ml_dtypes.bfloat16)


def column_map():
    u = np.zeros((2 * LANES, 2 * LANES))
    for j in range(LANES):
        u[j, 2 * j] += 0.375
        u[j, 2 * j + 1] += 0.375
        if j > 0:
            u[j - 1, 2 * j] += 0.125
        if j < LANES - 1:
            u[j + 1, 2 * j + 1] += 0.125
    u[LANES, 0] = 0.125
    u[LANES + 1, 2 * LANES - 1] = 0.125
    return u.astype(ml_dtypes.bfloat16)


def exact_dot(x, w):
    high = x.astype(jnp.bfloat16)
    rest = x - high.astype(jnp.float32)
    middle = rest.astype(jnp.bfloat16)
    low = (rest - middle.astype(jnp.float32)).astype(jnp.bfloat16)
    dot = functools.partial(jnp.dot, preferred_element_type=jnp.float32)
    return (dot(low, w) + dot(middle, w)) + dot(high, w)


def lanes_of(shape):
    return lax.broadcasted_iota(jnp.int32, shape, len(shape) - 1)


def tile_is_odd():
    return lax.axis_index("tile") % 2 == 1


def fetch(pad, refs, raw, sems):
    depth = refs[0].shape[0]
    sources = [(ref, 0, 0) for ref in refs[:2]]
    sources += [(ref, r, h) for ref in refs[2:] for r in range(2) for h in range(2)]
    copies = []
    for i, (ref, r, h) in enumerate(sources):
        source = ref.at[:, r, pl.ds(h * LANES, LANES)]
        copies.append(pltpu.make_async_copy(source, raw.at[pl.ds(i * pad, depth)], sems.at[i]))
    for copy in copies:
        copy.start()
    tail = jnp.zeros((pad - depth, LANES), jnp.float32)
    for i in range(len(sources)):
        raw[i * pad + depth : (i + 1) * pad, :] = tail
    for copy in copies:
        copy.wait()
    return [raw[i * pad : (i + 1) * pad, :] for i in range(len(sources))]


def put_rows(pad, target, planes, take_first):
    target[0:pad, :] = planes[0]
    target[pad : 2 * pad, :] = planes[1]
    for plane in range(2):
        for h in range(2):
            first, last = planes[2 + 4 * plane + h], planes[4 + 4 * plane + h]
            at = (2 + 2 * plane + h) * pad
            target[at : at + pad, :] = jnp.where(take_first, first, last)


def pack_kernel(pad, cc_ref, cs_ref, mc_ref, ms_ref, edge_ref, yrow_ref, xrow_ref, raw, sems):
    odd = tile_is_odd()
    planes = fetch(pad, (cc_ref, cs_ref, mc_ref, ms_ref), raw, sems)
    lane = lanes_of((pad, LANES))
    columns = jnp.zeros((pad, LANES), jnp.float32)
    for plane in range(2):
        m = planes[2 + 4 * plane : 6 + 4 * plane]
        cells = [(planes[plane], 0), (planes[plane], LANES - 1), (m[0], 0), (m[1], LANES - 1), (m[2], 0), (m[3], LANES - 1)]
        for e, (source, at) in enumerate(cells):
            out = plane * EDGES + e
            moved = pltpu.roll(source, (out - at) % LANES, 1) if out != at else source
            columns = jnp.where(lane == out, moved, columns)
    packed = columns[0:8]
    for i in range(1, pad // 8):
        packed = packed + pltpu.roll(columns[8 * i : 8 * i + 8], GROUP * i, 1)
    edge_ref[...] = packed
    for target, take_first in ((yrow_ref, jnp.logical_not(odd)), (xrow_ref, odd)):
        put_rows(pad, target, planes, take_first)
        target[6 * pad : 6 * pad + 8, :] = packed


def gather_kernel(pad, own_ref, y_ref, x_ref, out_ref):
    odd = tile_is_odd()
    from_x, from_y = x_ref[6 * pad : 6 * pad + 8, :], y_ref[6 * pad : 6 * pad + 8, :]
    out_ref[0:8, :] = jnp.where(odd, from_x, from_y)
    out_ref[8:16, :] = own_ref[...]
    out_ref[16:24, :] = jnp.where(odd, from_y, from_x)


def eliminate(depth, lo_ref, up_ref, stages):
    middle = depth // 2
    halves = (
        list(range(middle)),
        list(range(depth - 1, middle - 1, -1)),
    )
    before = [[None, None] for _ in stages]
    minor = [[None, None] for _ in stages]
    last = [[None, None] for _ in stages]
    for j in range(max(map(len, halves))):
        for side, levels in enumerate(halves):
            if j >= len(levels):
                continue
            k = levels[j]
            total = lo_ref[k] + up_ref[k]
            if j > 0:
                product = up_ref[k - 1] * lo_ref[k] if side == 0 else lo_ref[k + 1] * up_ref[k]
            toward = (lo_ref[k + 1] if side == 0 else up_ref[k - 1]) if 0 < k < depth - 1 or j == 0 else None
            for n, (shift_at, put_inverse, put_factor) in enumerate(stages):
                diagonal = shift_at(k) + total
                if j == 0:
                    here = diagonal
                    inverse = 1.0 / here
                elif j == 1:
                    here = diagonal * minor[n][side] - product
                    inverse = minor[n][side] / here
                else:
                    here = diagonal * minor[n][side] - product * before[n][side]
                    inverse = minor[n][side] / here
                before[n][side], minor[n][side] = minor[n][side], here
                last[n][side] = toward * inverse
                put_inverse(k, inverse)
                put_factor(k, last[n][side])
    for n, (_, _, put_factor) in enumerate(stages):
        put_factor(depth, 1.0 / (1.0 - last[n][0] * last[n][1]))


def solve(depth, lo_ref, up_ref, sets):
    middle = depth // 2
    top = [None] * len(sets)
    bottom = [None] * len(sets)
    for j in range(depth - middle):
        for n, (rhs, inverse, factor, put, get) in enumerate(sets):
            if j < middle:
                i = inverse(j)
                v = rhs(j) * i
                top[n] = v if j == 0 else v + (up_ref[j - 1] * i) * top[n]
                put(j, top[n])
            k = depth - 1 - j
            i = inverse(k)
            v = rhs(k) * i
            bottom[n] = v if j == 0 else v + (lo_ref[k + 1] * i) * bottom[n]
            if k > middle:
                put(k, bottom[n])
    for n, (rhs, inverse, factor, put, get) in enumerate(sets):
        bottom[n] = (bottom[n] + factor(middle) * top[n]) * factor(depth)
        top[n] = top[n] + factor(middle - 1) * bottom[n]
        put(middle, bottom[n])
        put(middle - 1, top[n])
    for j in range(1, depth - middle):
        for n, (rhs, inverse, factor, put, get) in enumerate(sets):
            k = middle - 1 - j
            if k >= 0:
                top[n] = get(k) + factor(k) * top[n]
                put(k, top[n])
            k = middle + j
            bottom[n] = get(k) + factor(k) * bottom[n]
            put(k, bottom[n])


def reader(ref, rows):
    return lambda k: ref[rows(k), :]


def writer(ref, rows):
    def put(k, v):
        ref[rows(k), :] = v

    return put


def plane_set(ref, ip, e, rows):
    return (reader(ref, rows), reader(ip, rows), reader(e, rows), writer(ref, rows), reader(ref, rows))


def block(pad, ref, i):
    return ref[i * pad : (i + 1) * pad, :]


def spaced(pad, count):
    return lambda k: pl.ds(k, count, stride=pad) if count > 1 else pl.ds(k, 1)


def prepare_rows(pad, depth, lo_ref, up_ref, ccot, cshift, mshift, cip, ce, mip, me, fine):
    c_rows, m_rows = spaced(pad, ccot.shape[0] // pad), spaced(pad, 4)
    eliminate(depth, lo_ref, up_ref, [
        (reader(cshift, c_rows), writer(cip, c_rows), writer(ce, c_rows)),
        (reader(mshift, m_rows), writer(mip, m_rows), writer(me, m_rows)),
    ] + fine)
    solve(depth, lo_ref, up_ref, [plane_set(ccot, cip, ce, c_rows)])
    tail = jnp.zeros((pad - depth, LANES), jnp.float32)
    for n in range(ccot.shape[0] // pad):
        ccot[n * pad + depth : (n + 1) * pad, :] = tail


def own_kernel(
    pad, lo_ref, up_ref, edge_ref, yown_ref, xown_ref, fs_ref,
    edge_out, ccot, mcot, mip, me, fip, fe,
    cshift, mshift, cip, ce,
):
    odd = tile_is_odd()
    edge_out[...] = edge_ref[...]
    ccot[...] = block(pad, xown_ref, 0)
    cshift[...] = block(pad, xown_ref, 1)
    for h in range(2):
        for i, target in ((2 + h, mcot), (4 + h, mshift)):
            in_x, in_y = block(pad, xown_ref, i), block(pad, yown_ref, i)
            target[h * pad : (1 + h) * pad, :] = jnp.where(odd, in_x, in_y)
            target[(2 + h) * pad : (3 + h) * pad, :] = jnp.where(odd, in_y, in_x)

    def put_fine(ref):
        def put(k, v):
            ref[k] = v

        return put

    fine = [(lambda k: fs_ref[k], put_fine(fip), put_fine(fe))]
    prepare_rows(pad, fs_ref.shape[0], lo_ref, up_ref, ccot, cshift, mshift, cip, ce, mip, me, fine)


def outer_kernel(
    pad, depth, flip_ref, lo_ref, up_ref, y_ref, x_ref,
    ccot, mcot, mip, me,
    cshift, mshift, cip, ce,
):
    t, tiles = lax.axis_index("tile"), lax.axis_size("tile")
    odd = tile_is_odd()
    back = (LANES - 1) - lanes_of((8, LANES))

    def reverse(x):
        return jnp.concatenate(
            [jnp.take_along_axis(x[8 * i : 8 * i + 8], back, axis=1) for i in range(pad // 8)], axis=0
        )

    for n in range(2):
        flip = flip_ref[lax.rem(t + tiles - 1, tiles) if n == 0 else t] == 1
        from_x = odd if n == 0 else jnp.logical_not(odd)
        plane = lambda i: jnp.where(from_x, block(pad, x_ref, i), block(pad, y_ref, i))
        for i, target in ((0, ccot), (1, cshift)):
            x = plane(i)
            target[n * pad : (n + 1) * pad, :] = jnp.where(flip, reverse(x), x)
        for i, target in ((2, mcot), (4, mshift)):
            x, y = plane(i), plane(i + 1)
            target[2 * n * pad : (2 * n + 1) * pad, :] = jnp.where(flip, reverse(y), x)
            target[(2 * n + 1) * pad : (2 * n + 2) * pad, :] = jnp.where(flip, reverse(x), y)
    prepare_rows(pad, depth, lo_ref, up_ref, ccot, cshift, mshift, cip, ce, mip, me, [])


def solve_kernel(
    pad, flip_ref, lo_ref, up_ref, c_own, m_own, ip_own, e_own, fip, fe, c_outer, m_outer, ip_outer, e_outer, fc_ref,
    own_ref, odd1_ref, odd_1_ref, even2_ref, even_2_ref, even_1_ref, even1_ref, odd2_ref, odd_2_ref, maps_ref, cols_ref,
    out_ref,
    ecot, eshift, eip, ee, mid, emid, xm, xf, fadd,
):
    depth = fc_ref.shape[0]
    t, s = lax.axis_index("tile"), lax.axis_index("strip")
    tiles, strips = lax.axis_size("tile"), lax.axis_size("strip")
    flips = flip_ref[lax.rem(t + tiles - 1, tiles)] * 2 + flip_ref[t]
    not_first, not_last = s > 0, s < strips - 1
    lane = lanes_of((pad, LANES))
    lane8 = lanes_of((8, LANES))
    tail = jnp.zeros((pad - depth, LANES), jnp.float32)

    packets = []
    for a in range(3):
        part = slice(8 * a, 8 * a + 8)
        packets += [
            (a - 1, -2, even2_ref[part, :] + odd2_ref[part, :]),
            (a - 1, -1, odd1_ref[part, :] + even1_ref[part, :]),
            (a - 1, 0, own_ref[part, :]),
            (a - 1, 1, odd_1_ref[part, :] + even_1_ref[part, :]),
            (a - 1, 2, even_2_ref[part, :] + odd_2_ref[part, :]),
        ]
    for i in range(pad // 8):
        cot = jnp.zeros((8, LANES), jnp.float32)
        shift = jnp.ones((8, LANES), jnp.float32)
        for a, b, packet in packets:
            at = edge_lane(a, b, 0)
            mask = (lane8 >= at) & (lane8 < at + EDGES)
            cot = jnp.where(mask, pltpu.roll(packet, (at - GROUP * i) % LANES, 1), cot)
            shift = jnp.where(mask, pltpu.roll(packet, (at - GROUP * i - EDGES) % LANES, 1), shift)
        ecot[8 * i : 8 * i + 8, :] = cot
        emid[8 * i : 8 * i + 8, :] = cot
        eshift[8 * i : 8 * i + 8, :] = shift

    one = lambda k: pl.ds(k, 1)
    eliminate(depth, lo_ref, up_ref, [(reader(eshift, one), writer(eip, one), writer(ee, one))])

    solve(depth, lo_ref, up_ref, [plane_set(ecot, eip, ee, one)])
    ecot[depth:, :] = tail
    c = [block(pad, c_outer, 0), c_own[...], block(pad, c_outer, 1)]
    edges = exact_dot(ecot[...], maps_ref[flips])
    for i, (main, other) in enumerate(((0, 1), (1, 0), (1, 2), (2, 1))):
        xm[i * pad : (i + 1) * pad, 0:LANES] = 0.375 * c[main] + 0.125 * c[other]
        sides = jnp.where(lane == 0, edges[:, 96 + 2 * i : 97 + 2 * i], 0.0)
        xm[i * pad : (i + 1) * pad, LANES:] = jnp.where(lane == 1, edges[:, 97 + 2 * i : 98 + 2 * i], sides)
    carried_rows = exact_dot(xm[...], cols_ref[...])
    place = (4, 0, 2, 6)
    for i in range(4):
        for h in range(2):
            at = place[i] + h
            raw = block(pad, m_own, at) if at < 4 else block(pad, m_outer, at - 4)
            mid[at * pad : (at + 1) * pad, :] = raw + block(pad, carried_rows, i)[:, h * LANES : (h + 1) * LANES]
    emid[...] = emid[...] + edges

    rows = spaced(pad, 4)
    outer = plane_set(mid, ip_outer, e_outer, lambda k: pl.ds(4 * pad + k, 4, stride=pad))
    outer = (outer[0], reader(ip_outer, rows), reader(e_outer, rows), outer[3], outer[4])
    solve(depth, lo_ref, up_ref, [plane_set(mid, ip_own, e_own, rows), outer, plane_set(emid, eip, ee, one)])
    for n in range(8):
        mid[n * pad + depth : (n + 1) * pad, :] = tail
    emid[depth:, :] = tail
    edges = exact_dot(emid[...], maps_ref[4 + flips])
    for i, (main, other) in enumerate(((1, 0), (1, 2), (2, 1), (2, 3))):
        halves = [
            0.375 * block(pad, mid, place[main] + h) + 0.125 * block(pad, mid, place[other] + h)
            for h in range(2)
        ]
        left = jnp.where(not_first, edges[:, 2 * i : 2 * i + 1], 0.0)
        right = jnp.where(not_last, edges[:, 2 * i + 1 : 2 * i + 2], 0.0)
        sides = ((left, halves[1][:, 0:1]), (halves[0][:, LANES - 1 :], right))
        for h in range(2):
            at = (2 * i + h) * pad
            xf[at : at + pad, 0:LANES] = halves[h]
            xf[at : at + pad, LANES:] = jnp.where(lane == 0, sides[h][0], jnp.where(lane == 1, sides[h][1], 0.0))
    carried_rows = exact_dot(xf[...], cols_ref[...])
    for i in range(4):
        for h in range(2):
            at = (2 * i + h) * pad
            for n in range(2):
                to = (4 * (2 * h + n) + i) * pad
                fadd[to : to + pad, :] = carried_rows[at : at + pad, n * LANES : (n + 1) * LANES]

    def fine_set(n):
        block = slice(n * LANES, (n + 1) * LANES)

        def put(k, v):
            out_ref[k, :, block] = v

        return (
            lambda k: fc_ref[k, :, block] + fadd[pl.ds(4 * n * pad + k, 4, stride=pad), :],
            lambda k: fip[k, :, block],
            lambda k: fe[k, :, block],
            put,
            lambda k: out_ref[k, :, block],
        )

    solve(depth, lo_ref, up_ref, [fine_set(n) for n in range(4)])


def moved(x, target):
    tiles, strips = lax.axis_size("tile"), lax.axis_size("strip")
    pairs = []
    for t in range(tiles):
        for s in range(strips):
            to = target(t, s)
            if to is not None and 0 <= to[1] < strips:
                pairs.append((t * strips + s, (to[0] % tiles) * strips + to[1]))
    return lax.ppermute(x, BOTH, pairs)


def on_device(fc, mc, cc, fs, ms, cs, lower, upper, seam_flip):
    depth = fc.shape[0]
    pad = (depth + 7) // 8 * 8
    f32 = jnp.float32
    array = lambda *shape: jax.ShapeDtypeStruct(shape, f32)
    scratch = lambda rows, width=LANES: pltpu.VMEM((rows * pad, width), f32)
    params = pltpu.CompilerParams(vmem_limit_bytes=24 * 1024 * 1024)
    fetched = [scratch(10), pltpu.SemaphoreType.DMA((10,))]
    fetching = pltpu.CompilerParams(vmem_limit_bytes=PACK_LIMIT)
    edge, yown, xown = pl.pallas_call(
        functools.partial(pack_kernel, pad),
        out_shape=(array(8, LANES), array(6 * pad + 8, LANES), array(6 * pad + 8, LANES)),
        in_specs=[ANY] * 4,
        out_specs=(VMEM,) * 3,
        scratch_shapes=[scratch(10), pltpu.SemaphoreType.DMA((10,))],
        compiler_params=pltpu.CompilerParams(vmem_limit_bytes=PACK_LIMIT),
    )(cc, cs, mc, ms)

    y = moved(yown, lambda t, s: (t + 1 if t % 2 else t - 1, s))
    x = moved(xown, lambda t, s: (t ^ 1, s))
    fine = array(*fc.shape)
    planes = lambda n: array(n * pad, LANES)
    edge, *own = pl.pallas_call(
        functools.partial(own_kernel, pad),
        out_shape=(array(8, LANES), planes(1), planes(4), planes(4), planes(4), fine, array(depth + 1, *fc.shape[1:])),
        in_specs=[SMEM] * 2 + [VMEM] * 4,
        out_specs=(VMEM,) * 7,
        scratch_shapes=[scratch(1), scratch(4), scratch(1), scratch(1)],
        compiler_params=params,
        cost_estimate=pl.CostEstimate(flops=20_000_000, bytes_accessed=4_000_000, transcendentals=0),
    )(lower, upper, edge, yown, xown, fs)
    columns = pl.pallas_call(
        functools.partial(gather_kernel, pad),
        out_shape=array(24, LANES),
        in_specs=[VMEM] * 3,
        out_specs=VMEM,
        compiler_params=params,
    )(edge, y, x)

    even = lambda step: moved(columns, lambda t, s: (t, s + step) if s % 2 == 0 else None)
    odd = lambda step: moved(columns, lambda t, s: (t, s + step) if s % 2 else None)
    strips = [odd(1), odd(-1), even(2), even(-2), even(-1), even(1), odd(2), odd(-2)]
    outer = pl.pallas_call(
        functools.partial(outer_kernel, pad, depth),
        out_shape=(planes(2), planes(4), planes(4), planes(4)),
        in_specs=[SMEM] * 3 + [VMEM] * 2,
        out_specs=(VMEM,) * 4,
        scratch_shapes=[scratch(2), scratch(4), scratch(2), scratch(2)],
        compiler_params=params,
        cost_estimate=pl.CostEstimate(flops=10_000_000, bytes_accessed=2_000_000, transcendentals=0),
    )(seam_flip, lower, upper, y, x)
    return pl.pallas_call(
        functools.partial(solve_kernel, pad),
        out_shape=fine,
        in_specs=[SMEM] * 3 + [VMEM] * 22,
        out_specs=VMEM,
        scratch_shapes=[scratch(1), scratch(1), scratch(1), scratch(1), scratch(8), scratch(1),
                        scratch(4, 2 * LANES), scratch(8, 2 * LANES), scratch(16)],
        compiler_params=params,
    )(seam_flip, lower, upper, *own, *outer, fc, columns, *strips,
      jnp.asarray(edge_maps()), jnp.asarray(column_map()))


def solution(mesh):
    field = P(None, "tile", "strip")
    return jax.shard_map(
        on_device, mesh=mesh, in_specs=(field,) * 6 + (P(),) * 3, out_specs=field, check_vma=False
    )
```

time: 849 us -> 55.6 us (0.07)
  the two profiles are of different devices: /device:TPU:36 before, /device:TPU:2 now
where the time goes in v1:
time: 55.6 us; the launch traced here: 55.1 us
  starting transfers between devices  44 us (79%)
  Pallas kernels  7.83 us (14%)
  local copies, waits for them, and re-layouts  2.96 us (5%)
    ppermute x10, starting transfers between devices, moved(): return lax.ppermute(x, BOTH, pairs)  44 us
    pallas_call x1, Pallas kernels, on_device(): pl.pallas_call(functools.partial(solve_kernel, pad), out_shape=fine, in_s...  3.76 us
    unnamed x20, local copies, waits for them, and re-layouts  2.96 us
    pallas_call x1, Pallas kernels, on_device(): pl.pallas_call(functools.partial(pack_kernel, pad), out_shape=(array(8, L...  2.01 us
  transfers between devices with their start and end apart: 10, of which 0 were waited for; matrix products, arithmetic and copies ran while one was open for 0% of the time, Pallas kernels for 4%

profile of v1, /device:TPU:2, one launch (start us, length us, event | category | flops | bytes accessed | tf_op | source)
XLA Modules:
  0.0 55.1 jit_solution(14235025192150860892)
XLA Ops:
  0.0 2.0 %shard_map.109 = (f32[8,128]{1,0:T(8,128)}, f32[440,128]{1,0:T(8,128)}, f32[440,128]{1,0:T(8,128)}) custom-call(f32[70,1,128]{2,1,0:T(1,128)} %cc_ref.1, f32[70,1,128]{2,1,0:T(1,128)} %cs_ref.1, f32[70,2,256]{2,1,0:T(2,128)} %mc_ref.1, f32[70,2,256]{2,1,0:T(2,128)} %ms_ref.1), custom_call_target="tpu_custom_call" | custom-call | tf_op jit(solution)/shard_map/pallas_call | solution.py:434
  2.0 18.7 %collective-permute-start = (f32[440,128]{1,0:T(8,128)}, f32[440,128]{1,0:T(8,128)S(1)}, u32[]{:S(2)}, u32[]{:S(2)}) collective-permute-start(f32[440,128]{1,0:T(8,128)} %get-tuple-element.20.yown_ref), channel_id=1, source_target_pairs={{0,1016},{1,1017},{2,1018},{3,1019},{4,1020},{5,1021},{6,1022},{7,... | collective-permute-start | bytes 675848 | tf_op jit(solution)/shard_map/ppermute | solution.py:422
  20.7 0.0 copy-start.6
  20.7 0.0 copy-start.7
  20.7 1.9 %collective-permute-start.1 = (f32[440,128]{1,0:T(8,128)}, f32[440,128]{1,0:T(8,128)S(1)}, u32[]{:S(2)}, u32[]{:S(2)}) collective-permute-start(f32[440,128]{1,0:T(8,128)} %get-tuple-element.21.xown_ref), channel_id=1, source_target_pairs={{0,8},{1,9},{2,10},{3,11},{4,12},{5,13},{6,14},{7,15},{8,0},{9,1},... | collective-permute-start | bytes 675848 | tf_op jit(solution)/shard_map/ppermute | solution.py:422
  22.7 0.0 copy-start
  22.7 1.1 %copy-done = f32[70,4,512]{2,1,0:T(4,128)S(1)} copy-done((f32[70,4,512]{2,1,0:T(4,128)S(1)}, f32[70,4,512]{2,1,0:T(4,128)}, u32[]{:S(2)}) %copy-start) | copy-done | bytes 573464
  23.8 0.9 %copy-done.3 = f32[440,128]{1,0:T(8,128)S(1)} copy-done((f32[440,128]{1,0:T(8,128)S(1)}, f32[440,128]{1,0:T(8,128)}, u32[]{:S(2)}) %copy-start.3) | copy-done | bytes 225304
  24.7 0.9 %copy-done.4 = f32[440,128]{1,0:T(8,128)S(1)} copy-done((f32[440,128]{1,0:T(8,128)S(1)}, f32[440,128]{1,0:T(8,128)}, u32[]{:S(2)}) %copy-start.4) | copy-done | bytes 225304
  25.6 1.0 %shard_map.110 = (f32[8,128]{1,0:T(8,128)S(1)}, f32[72,128]{1,0:T(8,128)S(1)}, f32[288,128]{1,0:T(8,128)S(1)}, f32[288,128]{1,0:T(8,128)S(1)}, f32[288,128]{1,0:...) custom-call(f32[70]{0:T(128)S(1)} %copy-done.6, f32[70]{0:T(128)S(1)} %copy-done.7, ...), custom_call_target="tpu_custom_call" | custom-call | flops 20000000 | bytes 4000000 | tf_op jit(solution)/shard_map/pallas_call | solution.py:447
  26.7 0.0 collective-permute-done.y_ref
  26.7 0.0 collective-permute-done.1.x_ref
  26.7 0.0 copy-start.2
  26.7 1.4 %collective-permute-start.2 = (f32[24,128]{1,0:T(8,128)S(1)}, f32[24,128]{1,0:T(8,128)S(1)}, u32[]{:S(2)}, u32[]{:S(2)}) collective-permute-start(f32[24,128]{1,0:T(8,128)S(1)} %shard_map.112.own_ref), channel_id=1, source_target_pairs={{1,2},{3,4},{5,6},{9,10},{11,12},{13,14},{17,18},{19,20},{21,22},{... | collective-permute-start | bytes 36872 | tf_op jit(solution)/shard_map/ppermute | solution.py:422
  28.2 1.3 %collective-permute-start.3 = (f32[24,128]{1,0:T(8,128)S(1)}, f32[24,128]{1,0:T(8,128)S(1)}, u32[]{:S(2)}, u32[]{:S(2)}) collective-permute-start(f32[24,128]{1,0:T(8,128)S(1)} %shard_map.112.own_ref), channel_id=1, source_target_pairs={{1,0},{3,2},{5,4},{7,6},{9,8},{11,10},{13,12},{15,14},{17,16},{19,... | collective-permute-start | bytes 36872 | tf_op jit(solution)/shard_map/ppermute | solution.py:422
  29.5 3.4 %collective-permute-start.4 = (f32[24,128]{1,0:T(8,128)S(1)}, f32[24,128]{1,0:T(8,128)S(1)}, u32[]{:S(2)}, u32[]{:S(2)}) collective-permute-start(f32[24,128]{1,0:T(8,128)S(1)} %shard_map.112.own_ref), channel_id=1, source_target_pairs={{0,2},{2,4},{4,6},{8,10},{10,12},{12,14},{16,18},{18,20},{20,22},{... | collective-permute-start | bytes 36872 | tf_op jit(solution)/shard_map/ppermute | solution.py:422
  32.9 3.9 %collective-permute-start.5 = (f32[24,128]{1,0:T(8,128)S(1)}, f32[24,128]{1,0:T(8,128)S(1)}, u32[]{:S(2)}, u32[]{:S(2)}) collective-permute-start(f32[24,128]{1,0:T(8,128)S(1)} %shard_map.112.own_ref), channel_id=1, source_target_pairs={{2,0},{4,2},{6,4},{10,8},{12,10},{14,12},{18,16},{20,18},{22,20},{... | collective-permute-start | bytes 36872 | tf_op jit(solution)/shard_map/ppermute | solution.py:422
  36.8 10.8 %collective-permute-start.6 = (f32[24,128]{1,0:T(8,128)S(1)}, f32[24,128]{1,0:T(8,128)S(1)}, u32[]{:S(2)}, u32[]{:S(2)}) collective-permute-start(f32[24,128]{1,0:T(8,128)S(1)} %shard_map.112.own_ref), channel_id=1, source_target_pairs={{2,1},{4,3},{6,5},{10,9},{12,11},{14,13},{18,17},{20,19},{22,21},{... | collective-permute-start | bytes 36872 | tf_op jit(solution)/shard_map/ppermute | solution.py:422
  47.6 0.0 collective-permute-done.2.odd1_ref
  47.6 1.3 %collective-permute-start.7 = (f32[24,128]{1,0:T(8,128)S(1)}, f32[24,128]{1,0:T(8,128)S(1)}, u32[]{:S(2)}, u32[]{:S(2)}) collective-permute-start(f32[24,128]{1,0:T(8,128)S(1)} %shard_map.112.own_ref), channel_id=1, source_target_pairs={{0,1},{2,3},{4,5},{6,7},{8,9},{10,11},{12,13},{14,15},{16,17},{18,... | collective-permute-start | bytes 36872 | tf_op jit(solution)/shard_map/ppermute | solution.py:422
  48.9 0.7 %collective-permute-start.8 = (f32[24,128]{1,0:T(8,128)S(1)}, f32[24,128]{1,0:T(8,128)S(1)}, u32[]{:S(2)}, u32[]{:S(2)}) collective-permute-start(f32[24,128]{1,0:T(8,128)S(1)} %shard_map.112.own_ref), channel_id=1, source_target_pairs={{1,3},{3,5},{5,7},{9,11},{11,13},{13,15},{17,19},{19,21},{21,23},{... | collective-permute-start | bytes 36872 | tf_op jit(solution)/shard_map/ppermute | solution.py:422
  49.6 0.7 %collective-permute-start.9 = (f32[24,128]{1,0:T(8,128)S(1)}, f32[24,128]{1,0:T(8,128)S(1)}, u32[]{:S(2)}, u32[]{:S(2)}) collective-permute-start(f32[24,128]{1,0:T(8,128)S(1)} %shard_map.112.own_ref), channel_id=1, source_target_pairs={{3,1},{5,3},{7,5},{11,9},{13,11},{15,13},{19,17},{21,19},{23,21},{... | collective-permute-start | bytes 36872 | tf_op jit(solution)/shard_map/ppermute | solution.py:422
  50.3 1.0 %shard_map.111 = (f32[144,128]{1,0:T(8,128)S(1)}, f32[288,128]{1,0:T(8,128)S(1)}, f32[288,128]{1,0:T(8,128)S(1)}, f32[288,128]{1,0:T(8,128)S(1)}) custom-call(s32[128]{0:T(128)S(1)} %copy-done.9, f32[70]{0:T(128)S(1)} %copy-done.6, f32[70]{0:T(128)S(1)} %copy-done.7, f32[440,128]{1,0:T(8,128)S(1)} %collective-permute-done.y_ref, ...), custom_call_target="tpu_custom_call" | custom-call | flops 10000000 | bytes 2000000 | tf_op jit(solution)/shard_map/pallas_call | solution.py:467
  51.4 3.8 %shard_map.113 = f32[70,4,512]{2,1,0:T(4,128)} custom-call(s32[128]{0:T(128)S(1)} %copy-done.9, f32[70]{0:T(128)S(1)} %copy-done.6, f32[70]{0:T(128)S(1)} %copy-done.7, f32[72,128]{1,0:T(8,128)S(1)} %get-tuple-element.22.c_own, f32[288,128]{1,0:T(8,128)S(1)} %get-tuple-element.23.m_own, f32[288,128]{1,0:T(8,128)S(1)} %get-tuple-element.24.ip_own, ...), custom_call_target="tpu_custom_call" | custom-call | tf_op jit(solution)/shard_map/pallas_call | solution.py:476
  (21 shorter events, 0.1 us)
Async XLA Ops:
  2.0 20.7 %copy-start.8 = (f32[8,128]{1,0:T(8,128)S(1)}, f32[8,128]{1,0:T(8,128)}, u32[]{:S(2)}) copy-start(f32[8,128]{1,0:T(8,128)} %get-tuple-element.19.edge_ref) | copy-start | bytes 12292
  2.0 24.6 %collective-permute-start = (f32[440,128]{1,0:T(8,128)}, f32[440,128]{1,0:T(8,128)S(1)}, u32[]{:S(2)}, u32[]{:S(2)}) collective-permute-start(f32[440,128]{1,0:T(8,128)} %get-tuple-element.20.yown_ref), channel_id=1, source_target_pairs={{0,1016},{1,1017},{2,1018},{3,1019},{4,1020},{5,1021},{6,1022},{7,... | collective-permute-start | bytes 675848 | tf_op jit(solution)/shard_map/ppermute | solution.py:422
  20.7 2.0 %copy-start.6 = (f32[70]{0:T(128)S(1)}, f32[70]{0:T(128)}, u32[]{:S(2)}) copy-start(f32[70]{0:T(128)} %lo_ref.5) | copy-start | bytes 844
  20.7 2.0 %copy-start.7 = (f32[70]{0:T(128)S(1)}, f32[70]{0:T(128)}, u32[]{:S(2)}) copy-start(f32[70]{0:T(128)} %up_ref.5) | copy-start | bytes 844
  20.7 5.9 %collective-permute-start.1 = (f32[440,128]{1,0:T(8,128)}, f32[440,128]{1,0:T(8,128)S(1)}, u32[]{:S(2)}, u32[]{:S(2)}) collective-permute-start(f32[440,128]{1,0:T(8,128)} %get-tuple-element.21.xown_ref), channel_id=1, source_target_pairs={{0,8},{1,9},{2,10},{3,11},{4,12},{5,13},{6,14},{7,15},{8,0},{9,1},... | collective-permute-start | bytes 675848 | tf_op jit(solution)/shard_map/ppermute | solution.py:422
  22.7 1.1 %copy-start = (f32[70,4,512]{2,1,0:T(4,128)S(1)}, f32[70,4,512]{2,1,0:T(4,128)}, u32[]{:S(2)}) copy-start(f32[70,4,512]{2,1,0:T(4,128)} %fs_ref.1) | copy-start | bytes 1720324
  23.8 0.9 %copy-start.3 = (f32[440,128]{1,0:T(8,128)S(1)}, f32[440,128]{1,0:T(8,128)}, u32[]{:S(2)}) copy-start(f32[440,128]{1,0:T(8,128)} %get-tuple-element.21.xown_ref) | copy-start | bytes 675844
  24.7 0.9 %copy-start.4 = (f32[440,128]{1,0:T(8,128)S(1)}, f32[440,128]{1,0:T(8,128)}, u32[]{:S(2)}) copy-start(f32[440,128]{1,0:T(8,128)} %get-tuple-element.20.yown_ref) | copy-start | bytes 675844
  25.6 24.6 %copy-start.9 = (s32[128]{0:T(128)S(1)}, s32[128]{0:T(128)}, u32[]{:S(2)}) copy-start(s32[128]{0:T(128)} %flip_ref.3) | copy-start | bytes 1540
  25.6 25.7 %copy-start.5 = (bf16[256,256]{1,0:T(8,128)(2,1)S(1)}, bf16[256,256]{1,0:T(8,128)(2,1)}, u32[]{:S(2)}) copy-start(bf16[256,256]{1,0:T(8,128)(2,1)} %constant.5.clone.cols_ref) | copy-start | bytes 393220
  26.7 24.7 %copy-start.1 = (f32[70,4,512]{2,1,0:T(4,128)S(1)}, f32[70,4,512]{2,1,0:T(4,128)}, u32[]{:S(2)}) copy-start(f32[70,4,512]{2,1,0:T(4,128)} %fc_ref.1) | copy-start | bytes 1720324
  26.7 24.7 %copy-start.2 = (bf16[8,128,128]{2,1,0:T(8,128)(2,1)S(1)}, bf16[8,128,128]{2,1,0:T(8,128)(2,1)}, u32[]{:S(2)}) copy-start(bf16[8,128,128]{2,1,0:T(8,128)(2,1)} %constant.4.clone.maps_ref) | copy-start | bytes 786436
  26.7 20.9 %collective-permute-start.2 = (f32[24,128]{1,0:T(8,128)S(1)}, f32[24,128]{1,0:T(8,128)S(1)}, u32[]{:S(2)}, u32[]{:S(2)}) collective-permute-start(f32[24,128]{1,0:T(8,128)S(1)} %shard_map.112.own_ref), channel_id=1, source_target_pairs={{1,2},{3,4},{5,6},{9,10},{11,12},{13,14},{17,18},{19,20},{21,22},{... | collective-permute-start | bytes 36872 | tf_op jit(solution)/shard_map/ppermute | solution.py:422
  28.2 20.7 %collective-permute-start.3 = (f32[24,128]{1,0:T(8,128)S(1)}, f32[24,128]{1,0:T(8,128)S(1)}, u32[]{:S(2)}, u32[]{:S(2)}) collective-permute-start(f32[24,128]{1,0:T(8,128)S(1)} %shard_map.112.own_ref), channel_id=1, source_target_pairs={{1,0},{3,2},{5,4},{7,6},{9,8},{11,10},{13,12},{15,14},{17,16},{19,... | collective-permute-start | bytes 36872 | tf_op jit(solution)/shard_map/ppermute | solution.py:422
  29.5 20.1 %collective-permute-start.4 = (f32[24,128]{1,0:T(8,128)S(1)}, f32[24,128]{1,0:T(8,128)S(1)}, u32[]{:S(2)}, u32[]{:S(2)}) collective-permute-start(f32[24,128]{1,0:T(8,128)S(1)} %shard_map.112.own_ref), channel_id=1, source_target_pairs={{0,2},{2,4},{4,6},{8,10},{10,12},{12,14},{16,18},{18,20},{20,22},{... | collective-permute-start | bytes 36872 | tf_op jit(solution)/shard_map/ppermute | solution.py:422
  32.9 18.4 %collective-permute-start.5 = (f32[24,128]{1,0:T(8,128)S(1)}, f32[24,128]{1,0:T(8,128)S(1)}, u32[]{:S(2)}, u32[]{:S(2)}) collective-permute-start(f32[24,128]{1,0:T(8,128)S(1)} %shard_map.112.own_ref), channel_id=1, source_target_pairs={{2,0},{4,2},{6,4},{10,8},{12,10},{14,12},{18,16},{20,18},{22,20},{... | collective-permute-start | bytes 36872 | tf_op jit(solution)/shard_map/ppermute | solution.py:422
  36.8 14.5 %collective-permute-start.6 = (f32[24,128]{1,0:T(8,128)S(1)}, f32[24,128]{1,0:T(8,128)S(1)}, u32[]{:S(2)}, u32[]{:S(2)}) collective-permute-start(f32[24,128]{1,0:T(8,128)S(1)} %shard_map.112.own_ref), channel_id=1, source_target_pairs={{2,1},{4,3},{6,5},{10,9},{12,11},{14,13},{18,17},{20,19},{22,21},{... | collective-permute-start | bytes 36872 | tf_op jit(solution)/shard_map/ppermute | solution.py:422
  47.6 3.7 %collective-permute-start.7 = (f32[24,128]{1,0:T(8,128)S(1)}, f32[24,128]{1,0:T(8,128)S(1)}, u32[]{:S(2)}, u32[]{:S(2)}) collective-permute-start(f32[24,128]{1,0:T(8,128)S(1)} %shard_map.112.own_ref), channel_id=1, source_target_pairs={{0,1},{2,3},{4,5},{6,7},{8,9},{10,11},{12,13},{14,15},{16,17},{18,... | collective-permute-start | bytes 36872 | tf_op jit(solution)/shard_map/ppermute | solution.py:422
  48.9 2.4 %collective-permute-start.8 = (f32[24,128]{1,0:T(8,128)S(1)}, f32[24,128]{1,0:T(8,128)S(1)}, u32[]{:S(2)}, u32[]{:S(2)}) collective-permute-start(f32[24,128]{1,0:T(8,128)S(1)} %shard_map.112.own_ref), channel_id=1, source_target_pairs={{1,3},{3,5},{5,7},{9,11},{11,13},{13,15},{17,19},{19,21},{21,23},{... | collective-permute-start | bytes 36872 | tf_op jit(solution)/shard_map/ppermute | solution.py:422
  49.6 1.8 %collective-permute-start.9 = (f32[24,128]{1,0:T(8,128)S(1)}, f32[24,128]{1,0:T(8,128)S(1)}, u32[]{:S(2)}, u32[]{:S(2)}) collective-permute-start(f32[24,128]{1,0:T(8,128)S(1)} %shard_map.112.own_ref), channel_id=1, source_target_pairs={{3,1},{5,3},{7,5},{11,9},{13,11},{15,13},{19,17},{21,19},{23,21},{... | collective-permute-start | bytes 36872 | tf_op jit(solution)/shard_map/ppermute | solution.py:422

commit v2 on v1

--- a/solution.py
+++ b/solution.py
@@ -12,6 +12,7 @@
 LANES = 128
 GROUP = 14
 PACK_LIMIT = 60 * 1024 * 1024
+PLACE = (4, 0, 2, 6)
 EDGES = 6
 BOTH = ("tile", "strip")
 VMEM = pl.BlockSpec(memory_space=pltpu.VMEM)
@@ -281,14 +282,18 @@
     prepare_rows(pad, fs_ref.shape[0], lo_ref, up_ref, ccot, cshift, mshift, cip, ce, mip, me, fine)
 
 
-def outer_kernel(
-    pad, depth, flip_ref, lo_ref, up_ref, y_ref, x_ref,
-    ccot, mcot, mip, me,
-    cshift, mshift, cip, ce,
+def first_half(
+    pad, depth, flip_ref, lo_ref, up_ref, y_ref, x_ref, c_own, m_own, own_ref, sides, maps_ref, cols_ref,
+    mid, emid, eip, ee, ip_outer, e_outer,
+    ccot, cshift, mshift, cip, ce, ecot, eshift, xm,
 ):
     t, tiles = lax.axis_index("tile"), lax.axis_size("tile")
     odd = tile_is_odd()
-    back = (LANES - 1) - lanes_of((8, LANES))
+    flips = flip_ref[lax.rem(t + tiles - 1, tiles)] * 2 + flip_ref[t]
+    lane = lanes_of((pad, LANES))
+    lane8 = lanes_of((8, LANES))
+    back = (LANES - 1) - lane8
+    tail = jnp.zeros((pad - depth, LANES), jnp.float32)
 
     def reverse(x):
         return jnp.concatenate(
@@ -302,38 +307,15 @@
         for i, target in ((0, ccot), (1, cshift)):
             x = plane(i)
             target[n * pad : (n + 1) * pad, :] = jnp.where(flip, reverse(x), x)
-        for i, target in ((2, mcot), (4, mshift)):
+        for i, target, at in ((2, mid, 4 + 2 * n), (4, mshift, 2 * n)):
             x, y = plane(i), plane(i + 1)
-            target[2 * n * pad : (2 * n + 1) * pad, :] = jnp.where(flip, reverse(y), x)
-            target[(2 * n + 1) * pad : (2 * n + 2) * pad, :] = jnp.where(flip, reverse(x), y)
-    prepare_rows(pad, depth, lo_ref, up_ref, ccot, cshift, mshift, cip, ce, mip, me, [])
-
-
-def solve_kernel(
-    pad, flip_ref, lo_ref, up_ref, c_own, m_own, ip_own, e_own, fip, fe, c_outer, m_outer, ip_outer, e_outer, fc_ref,
-    own_ref, odd1_ref, odd_1_ref, even2_ref, even_2_ref, even_1_ref, even1_ref, odd2_ref, odd_2_ref, maps_ref, cols_ref,
-    out_ref,
-    ecot, eshift, eip, ee, mid, emid, xm, xf, fadd,
-):
-    depth = fc_ref.shape[0]
-    t, s = lax.axis_index("tile"), lax.axis_index("strip")
-    tiles, strips = lax.axis_size("tile"), lax.axis_size("strip")
-    flips = flip_ref[lax.rem(t + tiles - 1, tiles)] * 2 + flip_ref[t]
-    not_first, not_last = s > 0, s < strips - 1
-    lane = lanes_of((pad, LANES))
-    lane8 = lanes_of((8, LANES))
-    tail = jnp.zeros((pad - depth, LANES), jnp.float32)
+            target[at * pad : (at + 1) * pad, :] = jnp.where(flip, reverse(y), x)
+            target[(at + 1) * pad : (at + 2) * pad, :] = jnp.where(flip, reverse(x), y)
 
     packets = []
     for a in range(3):
         part = slice(8 * a, 8 * a + 8)
-        packets += [
-            (a - 1, -2, even2_ref[part, :] + odd2_ref[part, :]),
-            (a - 1, -1, odd1_ref[part, :] + even1_ref[part, :]),
-            (a - 1, 0, own_ref[part, :]),
-            (a - 1, 1, odd_1_ref[part, :] + even_1_ref[part, :]),
-            (a - 1, 2, even_2_ref[part, :] + odd_2_ref[part, :]),
-        ]
+        packets += [(a - 1, b, ref[part, :]) for b, ref in ((0, own_ref),) + sides]
     for i in range(pad // 8):
         cot = jnp.zeros((8, LANES), jnp.float32)
         shift = jnp.ones((8, LANES), jnp.float32)
@@ -346,27 +328,78 @@
         emid[8 * i : 8 * i + 8, :] = cot
         eshift[8 * i : 8 * i + 8, :] = shift
 
-    one = lambda k: pl.ds(k, 1)
-    eliminate(depth, lo_ref, up_ref, [(reader(eshift, one), writer(eip, one), writer(ee, one))])
-
-    solve(depth, lo_ref, up_ref, [plane_set(ecot, eip, ee, one)])
+    one, two, four = spaced(pad, 1), spaced(pad, 2), spaced(pad, 4)
+    eliminate(depth, lo_ref, up_ref, [
+        (reader(eshift, one), writer(eip, one), writer(ee, one)),
+        (reader(cshift, two), writer(cip, two), writer(ce, two)),
+        (reader(mshift, four), writer(ip_outer, four), writer(e_outer, four)),
+    ])
+
+    solve(depth, lo_ref, up_ref, [plane_set(ecot, eip, ee, one), plane_set(ccot, cip, ce, two)])
     ecot[depth:, :] = tail
-    c = [block(pad, c_outer, 0), c_own[...], block(pad, c_outer, 1)]
+    for n in range(2):
+        ccot[n * pad + depth : (n + 1) * pad, :] = tail
+    c = [block(pad, ccot, 0), c_own[...], block(pad, ccot, 1)]
     edges = exact_dot(ecot[...], maps_ref[flips])
     for i, (main, other) in enumerate(((0, 1), (1, 0), (1, 2), (2, 1))):
         xm[i * pad : (i + 1) * pad, 0:LANES] = 0.375 * c[main] + 0.125 * c[other]
-        sides = jnp.where(lane == 0, edges[:, 96 + 2 * i : 97 + 2 * i], 0.0)
-        xm[i * pad : (i + 1) * pad, LANES:] = jnp.where(lane == 1, edges[:, 97 + 2 * i : 98 + 2 * i], sides)
+        left = jnp.where(lane == 0, edges[:, 96 + 2 * i : 97 + 2 * i], 0.0)
+        xm[i * pad : (i + 1) * pad, LANES:] = jnp.where(lane == 1, edges[:, 97 + 2 * i : 98 + 2 * i], left)
     carried_rows = exact_dot(xm[...], cols_ref[...])
-    place = (4, 0, 2, 6)
     for i in range(4):
         for h in range(2):
-            at = place[i] + h
-            raw = block(pad, m_own, at) if at < 4 else block(pad, m_outer, at - 4)
+            at = PLACE[i] + h
+            raw = block(pad, m_own if at < 4 else mid, at)
             mid[at * pad : (at + 1) * pad, :] = raw + block(pad, carried_rows, i)[:, h * LANES : (h + 1) * LANES]
     emid[...] = emid[...] + edges
 
-    rows = spaced(pad, 4)
+
+def even_kernel(
+    pad, depth, flip_ref, lo_ref, up_ref, y_ref, x_ref, c_own, m_own, own_ref,
+    even_2_ref, even2_ref, odd_1_ref, odd1_ref, maps_ref, cols_ref, *refs,
+):
+    sides = ((-2, even2_ref), (-1, odd1_ref), (1, odd_1_ref), (2, even_2_ref))
+
+    @pl.when(lax.axis_index("strip") % 2 == 0)
+    def _():
+        first_half(
+            pad, depth, flip_ref, lo_ref, up_ref, y_ref, x_ref, c_own, m_own, own_ref, sides, maps_ref, cols_ref, *refs
+        )
+
+
+def solve_kernel(
+    pad, flip_ref, lo_ref, up_ref, y_ref, x_ref, c_own, m_own, own_ref,
+    odd_2_ref, odd2_ref, even1_ref, even_1_ref, maps_ref, cols_ref,
+    mid_ref, emid_ref, eip_ref, ee_ref, ip_outer_ref, e_outer_ref, ip_own, e_own, fip, fe, fc_ref,
+    out_ref,
+    mid, emid, eip, ee, ip_outer, e_outer,
+    ccot, cshift, mshift, cip, ce, ecot, eshift, xm, xf, fadd,
+):
+    depth = fc_ref.shape[0]
+    t, s = lax.axis_index("tile"), lax.axis_index("strip")
+    tiles, strips = lax.axis_size("tile"), lax.axis_size("strip")
+    flips = flip_ref[lax.rem(t + tiles - 1, tiles)] * 2 + flip_ref[t]
+    not_first, not_last = s > 0, s < strips - 1
+    lane = lanes_of((pad, LANES))
+    tail = jnp.zeros((pad - depth, LANES), jnp.float32)
+
+    @pl.when(s % 2 == 0)
+    def _():
+        for target, source in (
+            (mid, mid_ref), (emid, emid_ref), (eip, eip_ref), (ee, ee_ref), (ip_outer, ip_outer_ref), (e_outer, e_outer_ref)
+        ):
+            target[...] = source[...]
+
+    @pl.when(s % 2 == 1)
+    def _():
+        sides = ((-2, odd2_ref), (-1, even1_ref), (1, even_1_ref), (2, odd_2_ref))
+        first_half(
+            pad, depth, flip_ref, lo_ref, up_ref, y_ref, x_ref, c_own, m_own, own_ref, sides, maps_ref, cols_ref,
+            mid, emid, eip, ee, ip_outer, e_outer,
+            ccot, cshift, mshift, cip, ce, ecot, eshift, xm,
+        )
+
+    one, rows = spaced(pad, 1), spaced(pad, 4)
     outer = plane_set(mid, ip_outer, e_outer, lambda k: pl.ds(4 * pad + k, 4, stride=pad))
     outer = (outer[0], reader(ip_outer, rows), reader(e_outer, rows), outer[3], outer[4])
     solve(depth, lo_ref, up_ref, [plane_set(mid, ip_own, e_own, rows), outer, plane_set(emid, eip, ee, one)])
@@ -376,7 +409,7 @@
     edges = exact_dot(emid[...], maps_ref[4 + flips])
     for i, (main, other) in enumerate(((1, 0), (1, 2), (2, 1), (2, 3))):
         halves = [
-            0.375 * block(pad, mid, place[main] + h) + 0.125 * block(pad, mid, place[other] + h)
+            0.375 * block(pad, mid, PLACE[main] + h) + 0.125 * block(pad, mid, PLACE[other] + h)
             for h in range(2)
         ]
         left = jnp.where(not_first, edges[:, 2 * i : 2 * i + 1], 0.0)
@@ -461,28 +494,33 @@
         compiler_params=params,
     )(edge, y, x)
 
-    even = lambda step: moved(columns, lambda t, s: (t, s + step) if s % 2 == 0 else None)
-    odd = lambda step: moved(columns, lambda t, s: (t, s + step) if s % 2 else None)
-    strips = [odd(1), odd(-1), even(2), even(-2), even(-1), even(1), odd(2), odd(-2)]
-    outer = pl.pallas_call(
-        functools.partial(outer_kernel, pad, depth),
-        out_shape=(planes(2), planes(4), planes(4), planes(4)),
-        in_specs=[SMEM] * 3 + [VMEM] * 2,
-        out_specs=(VMEM,) * 4,
-        scratch_shapes=[scratch(2), scratch(4), scratch(2), scratch(2)],
+    def send(x, parity, step):
+        return moved(x, lambda t, s: (t, s + step) if s % 2 == parity else None)
+
+    maps, cols = jnp.asarray(edge_maps()), jnp.asarray(column_map())
+    shared = [scratch(2), scratch(2), scratch(4), scratch(2), scratch(2), scratch(1), scratch(1), scratch(4, 2 * LANES)]
+    half_shapes = (8, 1, 1, 1, 4, 4)
+    c_own, m_own, *own = own
+    to_even = [send(columns, 0, -2), send(columns, 0, 2), send(columns, 1, -1), send(columns, 1, 1)]
+    half = pl.pallas_call(
+        functools.partial(even_kernel, pad, depth),
+        out_shape=tuple(planes(n) for n in half_shapes),
+        in_specs=[SMEM] * 3 + [VMEM] * 11,
+        out_specs=(VMEM,) * 6,
+        scratch_shapes=shared,
         compiler_params=params,
         cost_estimate=pl.CostEstimate(flops=10_000_000, bytes_accessed=2_000_000, transcendentals=0),
-    )(seam_flip, lower, upper, y, x)
+    )(seam_flip, lower, upper, y, x, c_own, m_own, columns, *to_even, maps, cols)
+    late, half = lax.optimization_barrier((columns, half))
+    to_odd = [send(late, 1, -2), send(late, 1, 2), send(late, 0, 1), send(late, 0, -1)]
     return pl.pallas_call(
         functools.partial(solve_kernel, pad),
         out_shape=fine,
         in_specs=[SMEM] * 3 + [VMEM] * 22,
         out_specs=VMEM,
-        scratch_shapes=[scratch(1), scratch(1), scratch(1), scratch(1), scratch(8), scratch(1),
-                        scratch(4, 2 * LANES), scratch(8, 2 * LANES), scratch(16)],
+        scratch_shapes=[scratch(n) for n in half_shapes] + shared + [scratch(8, 2 * LANES), scratch(16)],
         compiler_params=params,
-    )(seam_flip, lower, upper, *own, *outer, fc, columns, *strips,
-      jnp.asarray(edge_maps()), jnp.asarray(column_map()))
+    )(seam_flip, lower, upper, y, x, c_own, m_own, columns, *to_odd, maps, cols, *half, *own, fc)
 
 
 def solution(mesh):

time: 55.6 us -> 54.3 us (0.977)
  starting transfers between devices: 44 us -> 36.3 us
  waiting for transfers between devices: 0.03 us -> 6.67 us
    ppermute x10, starting transfers between devices: 44 us -> 36.3 us  [moved(): return lax.ppermute(x, BOTH, pairs)]
    ppermute x10, waiting for transfers between devices: 0.03 us -> 6.67 us  [moved(): return lax.ppermute(x, BOTH, pairs)]
    pallas_call x1, Pallas kernels: 3.76 us -> 2.8 us  [on_device(): pl.pallas_call(functools.partial(solve_kernel, pad), out_shape=fine, in_s...]
    pallas_call x1, Pallas kernels: 1.02 us -> 1.75 us  [on_device(): pl.pallas_call(functools.partial(even_kernel, pad, depth), out_shape=tupl...]
  transfers between devices with their start and end apart: 10 -> 10, of which waited for: 0 -> 2; matrix products, arithmetic and copies ran while one was open for 0% -> 0% of each run, Pallas kernels for 4% -> 2%
where the time goes in v2:
time: 54.3 us; the launch traced here: 53.8 us
  starting transfers between devices  36.3 us (67%)
  Pallas kernels  7.59 us (14%)
  waiting for transfers between devices  6.67 us (12%)
  local copies, waits for them, and re-layouts  2.97 us (5%)
    ppermute x10, starting transfers between devices, moved(): return lax.ppermute(x, BOTH, pairs)  36.3 us
    ppermute x10, waiting for transfers between devices, moved(): return lax.ppermute(x, BOTH, pairs)  6.67 us
    unnamed x20, local copies, waits for them, and re-layouts  2.97 us
    pallas_call x1, Pallas kernels, on_device(): pl.pallas_call(functools.partial(solve_kernel, pad), out_shape=fine, in_s...  2.8 us
    pallas_call x1, Pallas kernels, on_device(): pl.pallas_call(functools.partial(pack_kernel, pad), out_shape=(array(8, L...  2.01 us
    pallas_call x1, Pallas kernels, on_device(): pl.pallas_call(functools.partial(even_kernel, pad, depth), out_shape=tupl...  1.75 us
  transfers between devices with their start and end apart: 10, of which 2 were waited for; matrix products, arithmetic and copies ran while one was open for 0% of the time, Pallas kernels for 2%

profile of v2, /device:TPU:2, one launch (start us, length us, event | category | flops | bytes accessed | tf_op | source)
XLA Modules:
  0.0 53.8 jit_solution(6953765964446122056)
XLA Ops:
  0.0 2.0 %shard_map.109 = (f32[8,128]{1,0:T(8,128)}, f32[440,128]{1,0:T(8,128)}, f32[440,128]{1,0:T(8,128)}) custom-call(f32[70,1,128]{2,1,0:T(1,128)} %cc_ref.1, f32[70,1,128]{2,1,0:T(1,128)} %cs_ref.1, f32[70,2,256]{2,1,0:T(2,128)} %mc_ref.1, f32[70,2,256]{2,1,0:T(2,128)} %ms_ref.1), custom_call_target="tpu_custom_call" | custom-call | tf_op jit(solution)/shard_map/pallas_call | solution.py:467
  2.0 18.7 %collective-permute-start = (f32[440,128]{1,0:T(8,128)}, f32[440,128]{1,0:T(8,128)S(1)}, u32[]{:S(2)}, u32[]{:S(2)}) collective-permute-start(f32[440,128]{1,0:T(8,128)} %get-tuple-element.28.yown_ref), channel_id=1, source_target_pairs={{0,1016},{1,1017},{2,1018},{3,1019},{4,1020},{5,1021},{6,1022},{7,... | collective-permute-start | bytes 675848 | tf_op jit(solution)/shard_map/ppermute | solution.py:455
  20.7 0.0 copy-start.6
  20.7 0.0 copy-start.7
  20.7 1.9 %collective-permute-start.1 = (f32[440,128]{1,0:T(8,128)}, f32[440,128]{1,0:T(8,128)S(1)}, u32[]{:S(2)}, u32[]{:S(2)}) collective-permute-start(f32[440,128]{1,0:T(8,128)} %get-tuple-element.29.xown_ref), channel_id=1, source_target_pairs={{0,8},{1,9},{2,10},{3,11},{4,12},{5,13},{6,14},{7,15},{8,0},{9,1},... | collective-permute-start | bytes 675848 | tf_op jit(solution)/shard_map/ppermute | solution.py:455
  22.7 1.1 %copy-done.2 = f32[70,4,512]{2,1,0:T(4,128)S(1)} copy-done((f32[70,4,512]{2,1,0:T(4,128)S(1)}, f32[70,4,512]{2,1,0:T(4,128)}, u32[]{:S(2)}) %copy-start.2) | copy-done | bytes 573464
  23.8 0.9 %copy-done.4 = f32[440,128]{1,0:T(8,128)S(1)} copy-done((f32[440,128]{1,0:T(8,128)S(1)}, f32[440,128]{1,0:T(8,128)}, u32[]{:S(2)}) %copy-start.4) | copy-done | bytes 225304
  24.7 0.9 %copy-done.5 = f32[440,128]{1,0:T(8,128)S(1)} copy-done((f32[440,128]{1,0:T(8,128)S(1)}, f32[440,128]{1,0:T(8,128)}, u32[]{:S(2)}) %copy-start.5) | copy-done | bytes 225304
  25.6 1.0 %shard_map.110 = (f32[8,128]{1,0:T(8,128)S(1)}, f32[72,128]{1,0:T(8,128)S(1)}, f32[288,128]{1,0:T(8,128)S(1)}, f32[288,128]{1,0:T(8,128)S(1)}, f32[288,128]{1,0:...) custom-call(f32[70]{0:T(128)S(1)} %copy-done.6, f32[70]{0:T(128)S(1)} %copy-done.7, ...), custom_call_target="tpu_custom_call" | custom-call | flops 20000000 | bytes 4000000 | tf_op jit(solution)/shard_map/pallas_call | solution.py:480
  26.7 0.0 copy-start.3
  26.7 0.0 copy-start.9
  26.7 1.4 %collective-permute-start.5 = (f32[24,128]{1,0:T(8,128)S(1)}, f32[24,128]{1,0:T(8,128)S(1)}, u32[]{:S(2)}, u32[]{:S(2)}) collective-permute-start(f32[24,128]{1,0:T(8,128)S(1)} %shard_map.111.own_ref), channel_id=1, source_target_pairs={{1,2},{3,4},{5,6},{9,10},{11,12},{13,14},{17,18},{19,20},{21,22},{... | collective-permute-start | bytes 36872 | tf_op jit(solution)/shard_map/ppermute | solution.py:455
  28.2 1.3 %collective-permute-start.4 = (f32[24,128]{1,0:T(8,128)S(1)}, f32[24,128]{1,0:T(8,128)S(1)}, u32[]{:S(2)}, u32[]{:S(2)}) collective-permute-start(f32[24,128]{1,0:T(8,128)S(1)} %shard_map.111.own_ref), channel_id=1, source_target_pairs={{1,0},{3,2},{5,4},{7,6},{9,8},{11,10},{13,12},{15,14},{17,16},{19,... | collective-permute-start | bytes 36872 | tf_op jit(solution)/shard_map/ppermute | solution.py:455
  29.5 3.4 %collective-permute-start.3 = (f32[24,128]{1,0:T(8,128)S(1)}, f32[24,128]{1,0:T(8,128)S(1)}, u32[]{:S(2)}, u32[]{:S(2)}) collective-permute-start(f32[24,128]{1,0:T(8,128)S(1)} %shard_map.111.own_ref), channel_id=1, source_target_pairs={{0,2},{2,4},{4,6},{8,10},{10,12},{12,14},{16,18},{18,20},{20,22},{... | collective-permute-start | bytes 36872 | tf_op jit(solution)/shard_map/ppermute | solution.py:455
  32.9 3.9 %collective-permute-start.2 = (f32[24,128]{1,0:T(8,128)S(1)}, f32[24,128]{1,0:T(8,128)S(1)}, u32[]{:S(2)}, u32[]{:S(2)}) collective-permute-start(f32[24,128]{1,0:T(8,128)S(1)} %shard_map.111.own_ref), channel_id=1, source_target_pairs={{2,0},{4,2},{6,4},{10,8},{12,10},{14,12},{18,16},{20,18},{22,20},{... | collective-permute-start | bytes 36872 | tf_op jit(solution)/shard_map/ppermute | solution.py:455
  36.8 5.3 %collective-permute-done.5.odd1_ref = f32[24,128]{1,0:T(8,128)S(1)} collective-permute-done((f32[24,128]{1,0:T(8,128)S(1)}, f32[24,128]{1,0:T(8,128)S(1)}, u32[]{:S(2)}, u32[]{:S(2)}) %collective-permute-start.5) | collective-permute-done | bytes 12320 | tf_op jit(solution)/shard_map/ppermute | solution.py:455
  42.1 1.3 %collective-permute-done.4.odd_1_ref = f32[24,128]{1,0:T(8,128)S(1)} collective-permute-done((f32[24,128]{1,0:T(8,128)S(1)}, f32[24,128]{1,0:T(8,128)S(1)}, u32[]{:S(2)}, u32[]{:S(2)}) %collective-permute-start.4) | collective-permute-done | bytes 12320 | tf_op jit(solution)/shard_map/ppermute | solution.py:455
  43.4 1.8 %shard_map.112 = (f32[576,128]{1,0:T(8,128)S(1)}, f32[72,128]{1,0:T(8,128)S(1)}, f32[72,128]{1,0:T(8,128)S(1)}, f32[72,128]{1,0:T(8,128)S(1)}, f32[288,128]{1,0:T(8,128)S(1)}, /*index=5*/f32[288,128]{1,0:T(8,128)S(1)}) custom-call(s32[128]{0:T(128)S(1)} %copy-done.9, f32[70]{0:T(128)S(1)} %copy-done.6, f32[70]{0:T(128)S(1)} %copy-done.7, ...), custom_call_target="tpu_custom_call" | custom-call | flops 10000000 | bytes 2000000 | tf_op jit(solution)/shard_map/pallas_call | solution.py:505
  45.2 3.1 %collective-permute-start.9 = (f32[24,128]{1,0:T(8,128)S(1)}, f32[24,128]{1,0:T(8,128)S(1)}, u32[]{:S(2)}, u32[]{:S(2)}) collective-permute-start(f32[24,128]{1,0:T(8,128)S(1)} %shard_map.111.own_ref), channel_id=1, source_target_pairs={{2,1},{4,3},{6,5},{10,9},{12,11},{14,13},{18,17},{20,19},{22,21},{... | collective-permute-start | bytes 36872 | tf_op jit(solution)/shard_map/ppermute | solution.py:455
  48.3 1.3 %collective-permute-start.8 = (f32[24,128]{1,0:T(8,128)S(1)}, f32[24,128]{1,0:T(8,128)S(1)}, u32[]{:S(2)}, u32[]{:S(2)}) collective-permute-start(f32[24,128]{1,0:T(8,128)S(1)} %shard_map.111.own_ref), channel_id=1, source_target_pairs={{0,1},{2,3},{4,5},{6,7},{8,9},{10,11},{12,13},{14,15},{16,17},{18,... | collective-permute-start | bytes 36872 | tf_op jit(solution)/shard_map/ppermute | solution.py:455
  49.6 0.7 %collective-permute-start.7 = (f32[24,128]{1,0:T(8,128)S(1)}, f32[24,128]{1,0:T(8,128)S(1)}, u32[]{:S(2)}, u32[]{:S(2)}) collective-permute-start(f32[24,128]{1,0:T(8,128)S(1)} %shard_map.111.own_ref), channel_id=1, source_target_pairs={{1,3},{3,5},{5,7},{9,11},{11,13},{13,15},{17,19},{19,21},{21,23},{... | collective-permute-start | bytes 36872 | tf_op jit(solution)/shard_map/ppermute | solution.py:455
  50.3 0.7 %collective-permute-start.6 = (f32[24,128]{1,0:T(8,128)S(1)}, f32[24,128]{1,0:T(8,128)S(1)}, u32[]{:S(2)}, u32[]{:S(2)}) collective-permute-start(f32[24,128]{1,0:T(8,128)S(1)} %shard_map.111.own_ref), channel_id=1, source_target_pairs={{3,1},{5,3},{7,5},{11,9},{13,11},{15,13},{19,17},{21,19},{23,21},{... | collective-permute-start | bytes 36872 | tf_op jit(solution)/shard_map/ppermute | solution.py:455
  50.9 0.0 collective-permute-done.8.even1_ref
  51.0 2.8 %shard_map.113 = f32[70,4,512]{2,1,0:T(4,128)} custom-call(s32[128]{0:T(128)S(1)} %copy-done.9, f32[70]{0:T(128)S(1)} %copy-done.6, f32[70]{0:T(128)S(1)} %copy-done.7, f32[440,128]{1,0:T(8,128)S(1)} %collective-permute-done.y_ref, f32[440,128]{1,0:T(8,128)S(1)} %collective-permute-done.1.x_ref, f32[72,128]{1,0:T(8,128)S(1)} %get-tuple-element.31.c_own, ...), custom_call_target="tpu_custom_call" | custom-call | tf_op jit(solution)/shard_map/pallas_call | solution.py:516
  (21 shorter events, 0.1 us)
Async XLA Ops:
  2.0 20.7 %copy-start.8 = (f32[8,128]{1,0:T(8,128)S(1)}, f32[8,128]{1,0:T(8,128)}, u32[]{:S(2)}) copy-start(f32[8,128]{1,0:T(8,128)} %get-tuple-element.30.edge_ref) | copy-start | bytes 12292
  2.0 24.6 %collective-permute-start = (f32[440,128]{1,0:T(8,128)}, f32[440,128]{1,0:T(8,128)S(1)}, u32[]{:S(2)}, u32[]{:S(2)}) collective-permute-start(f32[440,128]{1,0:T(8,128)} %get-tuple-element.28.yown_ref), channel_id=1, source_target_pairs={{0,1016},{1,1017},{2,1018},{3,1019},{4,1020},{5,1021},{6,1022},{7,... | collective-permute-start | bytes 675848 | tf_op jit(solution)/shard_map/ppermute | solution.py:455
  20.7 2.0 %copy-start.6 = (f32[70]{0:T(128)S(1)}, f32[70]{0:T(128)}, u32[]{:S(2)}) copy-start(f32[70]{0:T(128)} %lo_ref.5) | copy-start | bytes 844
  20.7 2.0 %copy-start.7 = (f32[70]{0:T(128)S(1)}, f32[70]{0:T(128)}, u32[]{:S(2)}) copy-start(f32[70]{0:T(128)} %up_ref.5) | copy-start | bytes 844
  20.7 5.9 %collective-permute-start.1 = (f32[440,128]{1,0:T(8,128)}, f32[440,128]{1,0:T(8,128)S(1)}, u32[]{:S(2)}, u32[]{:S(2)}) collective-permute-start(f32[440,128]{1,0:T(8,128)} %get-tuple-element.29.xown_ref), channel_id=1, source_target_pairs={{0,8},{1,9},{2,10},{3,11},{4,12},{5,13},{6,14},{7,15},{8,0},{9,1},... | collective-permute-start | bytes 675848 | tf_op jit(solution)/shard_map/ppermute | solution.py:455
  22.7 1.1 %copy-start.2 = (f32[70,4,512]{2,1,0:T(4,128)S(1)}, f32[70,4,512]{2,1,0:T(4,128)}, u32[]{:S(2)}) copy-start(f32[70,4,512]{2,1,0:T(4,128)} %fs_ref.1) | copy-start | bytes 1720324
  23.8 0.9 %copy-start.4 = (f32[440,128]{1,0:T(8,128)S(1)}, f32[440,128]{1,0:T(8,128)}, u32[]{:S(2)}) copy-start(f32[440,128]{1,0:T(8,128)} %get-tuple-element.29.xown_ref) | copy-start | bytes 675844
  24.7 0.9 %copy-start.5 = (f32[440,128]{1,0:T(8,128)S(1)}, f32[440,128]{1,0:T(8,128)}, u32[]{:S(2)}) copy-start(f32[440,128]{1,0:T(8,128)} %get-tuple-element.28.yown_ref) | copy-start | bytes 675844
  26.7 16.8 %copy-start = (bf16[8,128,128]{2,1,0:T(8,128)(2,1)S(1)}, bf16[8,128,128]{2,1,0:T(8,128)(2,1)}, u32[]{:S(2)}) copy-start(bf16[8,128,128]{2,1,0:T(8,128)(2,1)} %constant.4.clone.maps_ref) | copy-start | bytes 786436
  26.7 16.7 %copy-start.3 = (bf16[256,256]{1,0:T(8,128)(2,1)S(1)}, bf16[256,256]{1,0:T(8,128)(2,1)}, u32[]{:S(2)}) copy-start(bf16[256,256]{1,0:T(8,128)(2,1)} %constant.5.clone.cols_ref) | copy-start | bytes 393220
  26.7 16.7 %copy-start.9 = (s32[128]{0:T(128)S(1)}, s32[128]{0:T(128)}, u32[]{:S(2)}) copy-start(s32[128]{0:T(128)} %flip_ref.3) | copy-start | bytes 1540
  26.7 24.3 %copy-start.1 = (f32[70,4,512]{2,1,0:T(4,128)S(1)}, f32[70,4,512]{2,1,0:T(4,128)}, u32[]{:S(2)}) copy-start(f32[70,4,512]{2,1,0:T(4,128)} %fc_ref.1) | copy-start | bytes 1720324
  26.7 15.3 %collective-permute-start.5 = (f32[24,128]{1,0:T(8,128)S(1)}, f32[24,128]{1,0:T(8,128)S(1)}, u32[]{:S(2)}, u32[]{:S(2)}) collective-permute-start(f32[24,128]{1,0:T(8,128)S(1)} %shard_map.111.own_ref), channel_id=1, source_target_pairs={{1,2},{3,4},{5,6},{9,10},{11,12},{13,14},{17,18},{19,20},{21,22},{... | collective-permute-start | bytes 36872 | tf_op jit(solution)/shard_map/ppermute | solution.py:455
  28.2 15.2 %collective-permute-start.4 = (f32[24,128]{1,0:T(8,128)S(1)}, f32[24,128]{1,0:T(8,128)S(1)}, u32[]{:S(2)}, u32[]{:S(2)}) collective-permute-start(f32[24,128]{1,0:T(8,128)S(1)} %shard_map.111.own_ref), channel_id=1, source_target_pairs={{1,0},{3,2},{5,4},{7,6},{9,8},{11,10},{13,12},{15,14},{17,16},{19,... | collective-permute-start | bytes 36872 | tf_op jit(solution)/shard_map/ppermute | solution.py:455
  29.5 13.9 %collective-permute-start.3 = (f32[24,128]{1,0:T(8,128)S(1)}, f32[24,128]{1,0:T(8,128)S(1)}, u32[]{:S(2)}, u32[]{:S(2)}) collective-permute-start(f32[24,128]{1,0:T(8,128)S(1)} %shard_map.111.own_ref), channel_id=1, source_target_pairs={{0,2},{2,4},{4,6},{8,10},{10,12},{12,14},{16,18},{18,20},{20,22},{... | collective-permute-start | bytes 36872 | tf_op jit(solution)/shard_map/ppermute | solution.py:455
  32.9 10.5 %collective-permute-start.2 = (f32[24,128]{1,0:T(8,128)S(1)}, f32[24,128]{1,0:T(8,128)S(1)}, u32[]{:S(2)}, u32[]{:S(2)}) collective-permute-start(f32[24,128]{1,0:T(8,128)S(1)} %shard_map.111.own_ref), channel_id=1, source_target_pairs={{2,0},{4,2},{6,4},{10,8},{12,10},{14,12},{18,16},{20,18},{22,20},{... | collective-permute-start | bytes 36872 | tf_op jit(solution)/shard_map/ppermute | solution.py:455
  45.2 5.7 %collective-permute-start.9 = (f32[24,128]{1,0:T(8,128)S(1)}, f32[24,128]{1,0:T(8,128)S(1)}, u32[]{:S(2)}, u32[]{:S(2)}) collective-permute-start(f32[24,128]{1,0:T(8,128)S(1)} %shard_map.111.own_ref), channel_id=1, source_target_pairs={{2,1},{4,3},{6,5},{10,9},{12,11},{14,13},{18,17},{20,19},{22,21},{... | collective-permute-start | bytes 36872 | tf_op jit(solution)/shard_map/ppermute | solution.py:455
  48.3 2.7 %collective-permute-start.8 = (f32[24,128]{1,0:T(8,128)S(1)}, f32[24,128]{1,0:T(8,128)S(1)}, u32[]{:S(2)}, u32[]{:S(2)}) collective-permute-start(f32[24,128]{1,0:T(8,128)S(1)} %shard_map.111.own_ref), channel_id=1, source_target_pairs={{0,1},{2,3},{4,5},{6,7},{8,9},{10,11},{12,13},{14,15},{16,17},{18,... | collective-permute-start | bytes 36872 | tf_op jit(solution)/shard_map/ppermute | solution.py:455
  49.6 1.4 %collective-permute-start.7 = (f32[24,128]{1,0:T(8,128)S(1)}, f32[24,128]{1,0:T(8,128)S(1)}, u32[]{:S(2)}, u32[]{:S(2)}) collective-permute-start(f32[24,128]{1,0:T(8,128)S(1)} %shard_map.111.own_ref), channel_id=1, source_target_pairs={{1,3},{3,5},{5,7},{9,11},{11,13},{13,15},{17,19},{19,21},{21,23},{... | collective-permute-start | bytes 36872 | tf_op jit(solution)/shard_map/ppermute | solution.py:455
  50.3 0.7 %collective-permute-start.6 = (f32[24,128]{1,0:T(8,128)S(1)}, f32[24,128]{1,0:T(8,128)S(1)}, u32[]{:S(2)}, u32[]{:S(2)}) collective-permute-start(f32[24,128]{1,0:T(8,128)S(1)} %shard_map.111.own_ref), channel_id=1, source_target_pairs={{3,1},{5,3},{7,5},{11,9},{13,11},{15,13},{19,17},{21,19},{23,21},{... | collective-permute-start | bytes 36872 | tf_op jit(solution)/shard_map/ppermute | solution.py:455

commit v3 on v2

--- a/solution.py
+++ b/solution.py
@@ -356,12 +356,15 @@
 
 def even_kernel(
     pad, depth, flip_ref, lo_ref, up_ref, y_ref, x_ref, c_own, m_own, own_ref,
-    even_2_ref, even2_ref, odd_1_ref, odd1_ref, maps_ref, cols_ref, *refs,
+    even_2_ref, even2_ref, odd_1_ref, odd1_ref, maps_ref, cols_ref, low_ref, high_ref, *refs,
 ):
     sides = ((-2, even2_ref), (-1, odd1_ref), (1, odd_1_ref), (2, even_2_ref))
 
     @pl.when(lax.axis_index("strip") % 2 == 0)
     def _():
+        for target, beyond in ((low_ref, odd_1_ref), (high_ref, odd1_ref)):
+            target[0:24, :] = own_ref[...]
+            target[24:48, :] = beyond[...]
         first_half(
             pad, depth, flip_ref, lo_ref, up_ref, y_ref, x_ref, c_own, m_own, own_ref, sides, maps_ref, cols_ref, *refs
         )
@@ -369,7 +372,7 @@
 
 def solve_kernel(
     pad, flip_ref, lo_ref, up_ref, y_ref, x_ref, c_own, m_own, own_ref,
-    odd_2_ref, odd2_ref, even1_ref, even_1_ref, maps_ref, cols_ref,
+    even1_ref, even_1_ref, maps_ref, cols_ref,
     mid_ref, emid_ref, eip_ref, ee_ref, ip_outer_ref, e_outer_ref, ip_own, e_own, fip, fe, fc_ref,
     out_ref,
     mid, emid, eip, ee, ip_outer, e_outer,
@@ -392,7 +395,10 @@
 
     @pl.when(s % 2 == 1)
     def _():
-        sides = ((-2, odd2_ref), (-1, even1_ref), (1, even_1_ref), (2, odd_2_ref))
+        near, beyond = pl.ds(0, 24), pl.ds(24, 24)
+        sides = (
+            (-2, even1_ref.at[beyond]), (-1, even1_ref.at[near]), (1, even_1_ref.at[near]), (2, even_1_ref.at[beyond])
+        )
         first_half(
             pad, depth, flip_ref, lo_ref, up_ref, y_ref, x_ref, c_own, m_own, own_ref, sides, maps_ref, cols_ref,
             mid, emid, eip, ee, ip_outer, e_outer,
@@ -502,21 +508,20 @@
     half_shapes = (8, 1, 1, 1, 4, 4)
     c_own, m_own, *own = own
     to_even = [send(columns, 0, -2), send(columns, 0, 2), send(columns, 1, -1), send(columns, 1, 1)]
-    half = pl.pallas_call(
+    low, high, *half = pl.pallas_call(
         functools.partial(even_kernel, pad, depth),
-        out_shape=tuple(planes(n) for n in half_shapes),
+        out_shape=(array(48, LANES),) * 2 + tuple(planes(n) for n in half_shapes),
         in_specs=[SMEM] * 3 + [VMEM] * 11,
-        out_specs=(VMEM,) * 6,
+        out_specs=(VMEM,) * 8,
         scratch_shapes=shared,
         compiler_params=params,
         cost_estimate=pl.CostEstimate(flops=10_000_000, bytes_accessed=2_000_000, transcendentals=0),
     )(seam_flip, lower, upper, y, x, c_own, m_own, columns, *to_even, maps, cols)
-    late, half = lax.optimization_barrier((columns, half))
-    to_odd = [send(late, 1, -2), send(late, 1, 2), send(late, 0, 1), send(late, 0, -1)]
+    to_odd = [send(high, 0, 1), send(low, 0, -1)]
     return pl.pallas_call(
         functools.partial(solve_kernel, pad),
         out_shape=fine,
-        in_specs=[SMEM] * 3 + [VMEM] * 22,
+        in_specs=[SMEM] * 3 + [VMEM] * 20,
         out_specs=VMEM,
         scratch_shapes=[scratch(n) for n in half_shapes] + shared + [scratch(8, 2 * LANES), scratch(16)],
         compiler_params=params,

time: 54.3 us -> 54.3 us (level)
  waiting for transfers between devices: 6.67 us -> 8.12 us
  starting transfers between devices: 36.3 us -> 35 us
    ppermute x10 -> x8, waiting for transfers between devices: 6.67 us -> 8.12 us  [moved(): return lax.ppermute(x, BOTH, pairs)]
    ppermute x10 -> x8, starting transfers between devices: 36.3 us -> 35 us  [moved(): return lax.ppermute(x, BOTH, pairs)]
  transfers between devices with their start and end apart: 10 -> 8, of which waited for: 2 -> 3; matrix products, arithmetic and copies ran while one was open for 0% -> 0% of each run, Pallas kernels for 2% -> 2%
where the time goes in v3:
time: 54.3 us; the launch traced here: 53.9 us
  starting transfers between devices  35 us (64%)
  waiting for transfers between devices  8.12 us (15%)
  Pallas kernels  7.57 us (14%)
  local copies, waits for them, and re-layouts  2.97 us (5%)
    ppermute x8, starting transfers between devices, moved(): return lax.ppermute(x, BOTH, pairs)  35 us
    ppermute x8, waiting for transfers between devices, moved(): return lax.ppermute(x, BOTH, pairs)  8.12 us
    unnamed x20, local copies, waits for them, and re-layouts  2.97 us
    pallas_call x1, Pallas kernels, on_device(): pl.pallas_call(functools.partial(solve_kernel, pad), out_shape=fine, in_s...  2.78 us
    pallas_call x1, Pallas kernels, on_device(): pl.pallas_call(functools.partial(pack_kernel, pad), out_shape=(array(8, L...  2 us
    pallas_call x1, Pallas kernels, on_device(): pl.pallas_call(functools.partial(even_kernel, pad, depth), out_shape=(arr...  1.76 us
  transfers between devices with their start and end apart: 8, of which 3 were waited for; matrix products, arithmetic and copies ran while one was open for 0% of the time, Pallas kernels for 2%

profile of v3, /device:TPU:2, one launch (start us, length us, event | category | flops | bytes accessed | tf_op | source)
XLA Modules:
  0.0 53.9 jit_solution(9331026956008696913)
XLA Ops:
  0.0 2.0 %shard_map.109 = (f32[8,128]{1,0:T(8,128)}, f32[440,128]{1,0:T(8,128)}, f32[440,128]{1,0:T(8,128)}) custom-call(f32[70,1,128]{2,1,0:T(1,128)} %cc_ref.1, f32[70,1,128]{2,1,0:T(1,128)} %cs_ref.1, f32[70,2,256]{2,1,0:T(2,128)} %mc_ref.1, f32[70,2,256]{2,1,0:T(2,128)} %ms_ref.1), custom_call_target="tpu_custom_call" | custom-call | tf_op jit(solution)/shard_map/pallas_call | solution.py:473
  2.0 18.7 %collective-permute-start = (f32[440,128]{1,0:T(8,128)}, f32[440,128]{1,0:T(8,128)S(1)}, u32[]{:S(2)}, u32[]{:S(2)}) collective-permute-start(f32[440,128]{1,0:T(8,128)} %get-tuple-element.23.yown_ref), channel_id=1, source_target_pairs={{0,1016},{1,1017},{2,1018},{3,1019},{4,1020},{5,1021},{6,1022},{7,... | collective-permute-start | bytes 675848 | tf_op jit(solution)/shard_map/ppermute | solution.py:461
  20.7 0.0 copy-start.6
  20.7 0.0 copy-start.7
  20.7 1.9 %collective-permute-start.1 = (f32[440,128]{1,0:T(8,128)}, f32[440,128]{1,0:T(8,128)S(1)}, u32[]{:S(2)}, u32[]{:S(2)}) collective-permute-start(f32[440,128]{1,0:T(8,128)} %get-tuple-element.24.xown_ref), channel_id=1, source_target_pairs={{0,8},{1,9},{2,10},{3,11},{4,12},{5,13},{6,14},{7,15},{8,0},{9,1},... | collective-permute-start | bytes 675848 | tf_op jit(solution)/shard_map/ppermute | solution.py:461
  22.7 0.0 copy-start.2
  22.7 1.1 %copy-done.2 = f32[70,4,512]{2,1,0:T(4,128)S(1)} copy-done((f32[70,4,512]{2,1,0:T(4,128)S(1)}, f32[70,4,512]{2,1,0:T(4,128)}, u32[]{:S(2)}) %copy-start.2) | copy-done | bytes 573464
  23.8 0.9 %copy-done.4 = f32[440,128]{1,0:T(8,128)S(1)} copy-done((f32[440,128]{1,0:T(8,128)S(1)}, f32[440,128]{1,0:T(8,128)}, u32[]{:S(2)}) %copy-start.4) | copy-done | bytes 225304
  24.7 0.9 %copy-done.5 = f32[440,128]{1,0:T(8,128)S(1)} copy-done((f32[440,128]{1,0:T(8,128)S(1)}, f32[440,128]{1,0:T(8,128)}, u32[]{:S(2)}) %copy-start.5) | copy-done | bytes 225304
  25.6 1.0 %shard_map.110 = (f32[8,128]{1,0:T(8,128)S(1)}, f32[72,128]{1,0:T(8,128)S(1)}, f32[288,128]{1,0:T(8,128)S(1)}, f32[288,128]{1,0:T(8,128)S(1)}, f32[288,128]{1,0:...) custom-call(f32[70]{0:T(128)S(1)} %copy-done.6, f32[70]{0:T(128)S(1)} %copy-done.7, ...), custom_call_target="tpu_custom_call" | custom-call | flops 20000000 | bytes 4000000 | tf_op jit(solution)/shard_map/pallas_call | solution.py:486
  26.7 0.0 copy-start.3
  26.7 0.0 copy-start.9
  26.7 0.0 copy-start.1
  26.7 1.4 %collective-permute-start.5 = (f32[24,128]{1,0:T(8,128)S(1)}, f32[24,128]{1,0:T(8,128)S(1)}, u32[]{:S(2)}, u32[]{:S(2)}) collective-permute-start(f32[24,128]{1,0:T(8,128)S(1)} %shard_map.111.own_ref), channel_id=1, source_target_pairs={{1,2},{3,4},{5,6},{9,10},{11,12},{13,14},{17,18},{19,20},{21,22},{... | collective-permute-start | bytes 36872 | tf_op jit(solution)/shard_map/ppermute | solution.py:461
  28.2 1.3 %collective-permute-start.4 = (f32[24,128]{1,0:T(8,128)S(1)}, f32[24,128]{1,0:T(8,128)S(1)}, u32[]{:S(2)}, u32[]{:S(2)}) collective-permute-start(f32[24,128]{1,0:T(8,128)S(1)} %shard_map.111.own_ref), channel_id=1, source_target_pairs={{1,0},{3,2},{5,4},{7,6},{9,8},{11,10},{13,12},{15,14},{17,16},{19,... | collective-permute-start | bytes 36872 | tf_op jit(solution)/shard_map/ppermute | solution.py:461
  29.5 3.4 %collective-permute-start.3 = (f32[24,128]{1,0:T(8,128)S(1)}, f32[24,128]{1,0:T(8,128)S(1)}, u32[]{:S(2)}, u32[]{:S(2)}) collective-permute-start(f32[24,128]{1,0:T(8,128)S(1)} %shard_map.111.own_ref), channel_id=1, source_target_pairs={{0,2},{2,4},{4,6},{8,10},{10,12},{12,14},{16,18},{18,20},{20,22},{... | collective-permute-start | bytes 36872 | tf_op jit(solution)/shard_map/ppermute | solution.py:461
  32.9 3.9 %collective-permute-start.2 = (f32[24,128]{1,0:T(8,128)S(1)}, f32[24,128]{1,0:T(8,128)S(1)}, u32[]{:S(2)}, u32[]{:S(2)}) collective-permute-start(f32[24,128]{1,0:T(8,128)S(1)} %shard_map.111.own_ref), channel_id=1, source_target_pairs={{2,0},{4,2},{6,4},{10,8},{12,10},{14,12},{18,16},{20,18},{22,20},{... | collective-permute-start | bytes 36872 | tf_op jit(solution)/shard_map/ppermute | solution.py:461
  36.8 5.3 %collective-permute-done.5.odd1_ref = f32[24,128]{1,0:T(8,128)S(1)} collective-permute-done((f32[24,128]{1,0:T(8,128)S(1)}, f32[24,128]{1,0:T(8,128)S(1)}, u32[]{:S(2)}, u32[]{:S(2)}) %collective-permute-start.5) | collective-permute-done | bytes 12320 | tf_op jit(solution)/shard_map/ppermute | solution.py:461
  42.1 1.3 %collective-permute-done.4.odd_1_ref = f32[24,128]{1,0:T(8,128)S(1)} collective-permute-done((f32[24,128]{1,0:T(8,128)S(1)}, f32[24,128]{1,0:T(8,128)S(1)}, u32[]{:S(2)}, u32[]{:S(2)}) %collective-permute-start.4) | collective-permute-done | bytes 12320 | tf_op jit(solution)/shard_map/ppermute | solution.py:461
  43.4 1.8 %shard_map.112 = (f32[48,128]{1,0:T(8,128)S(1)}, f32[48,128]{1,0:T(8,128)S(1)}, f32[576,128]{1,0:T(8,128)S(1)}, f32[72,128]{1,0:T(8,128)S(1)}, f32[72,128]{1,0:T...) custom-call(s32[128]{0:T(128)S(1)} %copy-done.9, f32[70]{0:T(128)S(1)} %copy-done.6, ...), custom_call_target="tpu_custom_call" | custom-call | flops 10000000 | bytes 2000000 | tf_op jit(solution)/shard_map/pallas_call | solution.py:511
  45.2 1.3 %collective-permute-start.6 = (f32[48,128]{1,0:T(8,128)S(1)}, f32[48,128]{1,0:T(8,128)S(1)}, u32[]{:S(2)}, u32[]{:S(2)}) collective-permute-start(f32[48,128]{1,0:T(8,128)S(1)} %get-tuple-element.29), channel_id=1, source_target_pairs={{0,1},{2,3},{4,5},{6,7},{8,9},{10,11},{12,13},{14,15},{16,17},{18,... | collective-permute-start | bytes 73736 | tf_op jit(solution)/shard_map/ppermute | solution.py:461
  46.5 3.1 %collective-permute-start.7 = (f32[48,128]{1,0:T(8,128)S(1)}, f32[48,128]{1,0:T(8,128)S(1)}, u32[]{:S(2)}, u32[]{:S(2)}) collective-permute-start(f32[48,128]{1,0:T(8,128)S(1)} %get-tuple-element.30), channel_id=1, source_target_pairs={{2,1},{4,3},{6,5},{10,9},{12,11},{14,13},{18,17},{20,19},{22,21},{... | collective-permute-start | bytes 73736 | tf_op jit(solution)/shard_map/ppermute | solution.py:461
  49.6 1.5 %collective-permute-done.7.even_1_ref = f32[48,128]{1,0:T(8,128)S(1)} collective-permute-done((f32[48,128]{1,0:T(8,128)S(1)}, f32[48,128]{1,0:T(8,128)S(1)}, u32[]{:S(2)}, u32[]{:S(2)}) %collective-permute-start.7) | collective-permute-done | bytes 24608 | tf_op jit(solution)/shard_map/ppermute | solution.py:461
  51.1 2.8 %shard_map.113 = f32[70,4,512]{2,1,0:T(4,128)} custom-call(s32[128]{0:T(128)S(1)} %copy-done.9, f32[70]{0:T(128)S(1)} %copy-done.6, f32[70]{0:T(128)S(1)} %copy-done.7, f32[440,128]{1,0:T(8,128)S(1)} %collective-permute-done.y_ref, f32[440,128]{1,0:T(8,128)S(1)} %collective-permute-done.1.x_ref, f32[72,128]{1,0:T(8,128)S(1)} %get-tuple-element.26.c_own, ...), custom_call_target="tpu_custom_call" | custom-call | tf_op jit(solution)/shard_map/pallas_call | solution.py:521
  (17 shorter events, 0.1 us)
Async XLA Ops:
  2.0 20.7 %copy-start.8 = (f32[8,128]{1,0:T(8,128)S(1)}, f32[8,128]{1,0:T(8,128)}, u32[]{:S(2)}) copy-start(f32[8,128]{1,0:T(8,128)} %get-tuple-element.25.edge_ref) | copy-start | bytes 12292
  2.0 24.6 %collective-permute-start = (f32[440,128]{1,0:T(8,128)}, f32[440,128]{1,0:T(8,128)S(1)}, u32[]{:S(2)}, u32[]{:S(2)}) collective-permute-start(f32[440,128]{1,0:T(8,128)} %get-tuple-element.23.yown_ref), channel_id=1, source_target_pairs={{0,1016},{1,1017},{2,1018},{3,1019},{4,1020},{5,1021},{6,1022},{7,... | collective-permute-start | bytes 675848 | tf_op jit(solution)/shard_map/ppermute | solution.py:461
  20.7 2.0 %copy-start.6 = (f32[70]{0:T(128)S(1)}, f32[70]{0:T(128)}, u32[]{:S(2)}) copy-start(f32[70]{0:T(128)} %lo_ref.5) | copy-start | bytes 844
  20.7 2.0 %copy-start.7 = (f32[70]{0:T(128)S(1)}, f32[70]{0:T(128)}, u32[]{:S(2)}) copy-start(f32[70]{0:T(128)} %up_ref.5) | copy-start | bytes 844
  20.7 5.9 %collective-permute-start.1 = (f32[440,128]{1,0:T(8,128)}, f32[440,128]{1,0:T(8,128)S(1)}, u32[]{:S(2)}, u32[]{:S(2)}) collective-permute-start(f32[440,128]{1,0:T(8,128)} %get-tuple-element.24.xown_ref), channel_id=1, source_target_pairs={{0,8},{1,9},{2,10},{3,11},{4,12},{5,13},{6,14},{7,15},{8,0},{9,1},... | collective-permute-start | bytes 675848 | tf_op jit(solution)/shard_map/ppermute | solution.py:461
  22.7 1.1 %copy-start.2 = (f32[70,4,512]{2,1,0:T(4,128)S(1)}, f32[70,4,512]{2,1,0:T(4,128)}, u32[]{:S(2)}) copy-start(f32[70,4,512]{2,1,0:T(4,128)} %fs_ref.1) | copy-start | bytes 1720324
  23.8 0.9 %copy-start.4 = (f32[440,128]{1,0:T(8,128)S(1)}, f32[440,128]{1,0:T(8,128)}, u32[]{:S(2)}) copy-start(f32[440,128]{1,0:T(8,128)} %get-tuple-element.24.xown_ref) | copy-start | bytes 675844
  24.7 0.9 %copy-start.5 = (f32[440,128]{1,0:T(8,128)S(1)}, f32[440,128]{1,0:T(8,128)}, u32[]{:S(2)}) copy-start(f32[440,128]{1,0:T(8,128)} %get-tuple-element.23.yown_ref) | copy-start | bytes 675844
  26.6 16.8 %copy-start = (bf16[8,128,128]{2,1,0:T(8,128)(2,1)S(1)}, bf16[8,128,128]{2,1,0:T(8,128)(2,1)}, u32[]{:S(2)}) copy-start(bf16[8,128,128]{2,1,0:T(8,128)(2,1)} %constant.4.clone.maps_ref) | copy-start | bytes 786436
  26.7 16.7 %copy-start.3 = (bf16[256,256]{1,0:T(8,128)(2,1)S(1)}, bf16[256,256]{1,0:T(8,128)(2,1)}, u32[]{:S(2)}) copy-start(bf16[256,256]{1,0:T(8,128)(2,1)} %constant.5.clone.cols_ref) | copy-start | bytes 393220
  26.7 16.7 %copy-start.9 = (s32[128]{0:T(128)S(1)}, s32[128]{0:T(128)}, u32[]{:S(2)}) copy-start(s32[128]{0:T(128)} %flip_ref.3) | copy-start | bytes 1540
  26.7 24.4 %copy-start.1 = (f32[70,4,512]{2,1,0:T(4,128)S(1)}, f32[70,4,512]{2,1,0:T(4,128)}, u32[]{:S(2)}) copy-start(f32[70,4,512]{2,1,0:T(4,128)} %fc_ref.1) | copy-start | bytes 1720324
  26.7 15.3 %collective-permute-start.5 = (f32[24,128]{1,0:T(8,128)S(1)}, f32[24,128]{1,0:T(8,128)S(1)}, u32[]{:S(2)}, u32[]{:S(2)}) collective-permute-start(f32[24,128]{1,0:T(8,128)S(1)} %shard_map.111.own_ref), channel_id=1, source_target_pairs={{1,2},{3,4},{5,6},{9,10},{11,12},{13,14},{17,18},{19,20},{21,22},{... | collective-permute-start | bytes 36872 | tf_op jit(solution)/shard_map/ppermute | solution.py:461
  28.2 15.2 %collective-permute-start.4 = (f32[24,128]{1,0:T(8,128)S(1)}, f32[24,128]{1,0:T(8,128)S(1)}, u32[]{:S(2)}, u32[]{:S(2)}) collective-permute-start(f32[24,128]{1,0:T(8,128)S(1)} %shard_map.111.own_ref), channel_id=1, source_target_pairs={{1,0},{3,2},{5,4},{7,6},{9,8},{11,10},{13,12},{15,14},{17,16},{19,... | collective-permute-start | bytes 36872 | tf_op jit(solution)/shard_map/ppermute | solution.py:461
  29.5 13.9 %collective-permute-start.3 = (f32[24,128]{1,0:T(8,128)S(1)}, f32[24,128]{1,0:T(8,128)S(1)}, u32[]{:S(2)}, u32[]{:S(2)}) collective-permute-start(f32[24,128]{1,0:T(8,128)S(1)} %shard_map.111.own_ref), channel_id=1, source_target_pairs={{0,2},{2,4},{4,6},{8,10},{10,12},{12,14},{16,18},{18,20},{20,22},{... | collective-permute-start | bytes 36872 | tf_op jit(solution)/shard_map/ppermute | solution.py:461
  32.9 10.5 %collective-permute-start.2 = (f32[24,128]{1,0:T(8,128)S(1)}, f32[24,128]{1,0:T(8,128)S(1)}, u32[]{:S(2)}, u32[]{:S(2)}) collective-permute-start(f32[24,128]{1,0:T(8,128)S(1)} %shard_map.111.own_ref), channel_id=1, source_target_pairs={{2,0},{4,2},{6,4},{10,8},{12,10},{14,12},{18,16},{20,18},{22,20},{... | collective-permute-start | bytes 36872 | tf_op jit(solution)/shard_map/ppermute | solution.py:461
  45.2 4.4 %collective-permute-start.6 = (f32[48,128]{1,0:T(8,128)S(1)}, f32[48,128]{1,0:T(8,128)S(1)}, u32[]{:S(2)}, u32[]{:S(2)}) collective-permute-start(f32[48,128]{1,0:T(8,128)S(1)} %get-tuple-element.29), channel_id=1, source_target_pairs={{0,1},{2,3},{4,5},{6,7},{8,9},{10,11},{12,13},{14,15},{16,17},{18,... | collective-permute-start | bytes 73736 | tf_op jit(solution)/shard_map/ppermute | solution.py:461
  46.5 4.6 %collective-permute-start.7 = (f32[48,128]{1,0:T(8,128)S(1)}, f32[48,128]{1,0:T(8,128)S(1)}, u32[]{:S(2)}, u32[]{:S(2)}) collective-permute-start(f32[48,128]{1,0:T(8,128)S(1)} %get-tuple-element.30), channel_id=1, source_target_pairs={{2,1},{4,3},{6,5},{10,9},{12,11},{14,13},{18,17},{20,19},{22,21},{... | collective-permute-start | bytes 73736 | tf_op jit(solution)/shard_map/ppermute | solution.py:461
